TPU v7x, 32 devices: a whole 2x2x4 slice. The times are simulated.
32 devices in a mesh: wide: 8 (over z, y), narrow: 4 (over x, core).
Axes of the slice: x: 2, y: 2, z: 4, core: 2. Of those that a mesh axis runs over, the one named last changes fastest.
Arguments:
- rhs: float32 [128, 32, 128], P('wide', 'narrow'), may hold values from -4 to 6
- coefficient: float32 [128, 32, 128], P('wide', 'narrow'), may hold values from 0.125 to 8
- guess: float32 [128, 32, 128], P('wide', 'narrow'), may hold values from -6 to 6
Outputs:
- pressure: float32 [128, 32, 128], P('wide', 'narrow')
- residual: float32 [128, 32, 128], P('wide', 'narrow')
All inputs are finite; a program needn't handle non-finite values.
Results may differ from a plain program's by a relative error of at most 0.0003.
Values sent between devices are 32-bit elements; how exact they have to be, the bound alone decides.
A program may use at most 128 MiB of HBM per device.

v0:
```python
import jax
import jax.numpy as jnp
from jax import lax
from jax.sharding import PartitionSpec as P

ITERS = 20


def padded_2(block, sides, width):
    for axis, dim in sides:
        count = lax.axis_size(axis)
        forward = [(i, i + 1) for i in range(count - 1)]
        backward = [(target, source) for source, target in forward]
        low = lax.ppermute(
            lax.slice_in_dim(block, block.shape[dim] - width, None, axis=dim), axis, forward
        )
        high = lax.ppermute(lax.slice_in_dim(block, 0, width, axis=dim), axis, backward)
        block = jnp.concatenate([low, block, high], axis=dim)
    return block


def shifts(field):
    padded = jnp.pad(field, 1)
    return [
        padded[2:, 1:-1, 1:-1],
        padded[:-2, 1:-1, 1:-1],
        padded[1:-1, 2:, 1:-1],
        padded[1:-1, :-2, 1:-1],
        padded[1:-1, 1:-1, 2:],
        padded[1:-1, 1:-1, :-2],
    ]


def weights(conduct):
    faces = [0.5 * (conduct + other) for other in shifts(conduct)]
    total = faces[0]
    for face in faces[1:]:
        total = total + face
    return (faces, total)


def beside_all(faces, field):
    near = shifts(field)
    total = faces[0] * near[0]
    for index in range(1, 6):
        total = total + faces[index] * near[index]
    return total


def restrict(field):
    sx, sz, sy = field.shape
    return jnp.sum(field.reshape(sx // 2, 2, sz // 2, 2, sy // 2, 2), axis=(1, 3, 5)) * 0.125


def prolong(field):
    return jnp.repeat(jnp.repeat(jnp.repeat(field, 2, axis=0), 2, axis=1), 2, axis=2)


def trimmed(array):
    return array[1:-1, 1:-1]


def setup(conduct, source, scale):
    cells_x, cells_z, cells_y = conduct.shape
    extended = padded_2(jnp.stack([conduct, source]), (("wide", 1), ("narrow", 2)), 2)
    faces, diag = weights(extended[0])
    diag = jnp.where(diag > 0.0, diag, 1.0)
    glob_x = lax.axis_index("wide") * cells_x + jnp.arange(-2, cells_x + 2, dtype=jnp.int32)
    glob_z = lax.axis_index("narrow") * cells_z + jnp.arange(-2, cells_z + 2, dtype=jnp.int32)
    limit_x = cells_x * lax.axis_size("wide")
    limit_z = cells_z * lax.axis_size("narrow")
    inside = ((glob_x >= 0) & (glob_x < limit_x))[:, None, None] & (
        (glob_z >= 0) & (glob_z < limit_z)
    )[None, :, None]
    across = jnp.arange(cells_y, dtype=jnp.int32)
    colour = (glob_x[:, None, None] + glob_z[None, :, None] + across[None, None, :]) % 2
    return (faces, diag, extended[1], inside, colour, scale)


def smooth(field, level):
    faces, diag, source, inside, colour, scale = level
    inner_faces = [trimmed(face) for face in faces]
    inner_diag = trimmed(diag)
    inner_source = trimmed(source) / scale
    inner_colour = trimmed(colour)
    for sweep in range(2):
        for parity in (0, 1):
            wider = padded_2(field, (("wide", 0), ("narrow", 1)), 1)
            fresh = (inner_source + beside_all(inner_faces, wider)) / inner_diag
            field = trimmed(jnp.where(inner_colour == parity, fresh, wider))
    return field


def defect(field, level):
    faces, diag, source, inside, colour, scale = level
    inner_faces = [trimmed(face) for face in faces]
    wider = padded_2(field, (("wide", 0), ("narrow", 1)), 1)
    result = trimmed(source) - scale * (trimmed(diag) * wider - beside_all(inner_faces, wider))
    return trimmed(result)


def bottom(source, faces, diag, scale):

    def advance(step, carry):
        answer, remain, search, norm_now = carry
        image = scale * (diag * search - beside_all(faces, search))
        alpha = norm_now / jnp.sum(search * image)
        answer = answer + alpha * search
        remain = remain - alpha * image
        norm_next = jnp.sum(remain * remain)
        search = remain + norm_next / norm_now * search
        return (answer, remain, search, norm_next)

    start = (jnp.zeros_like(source), source, source, jnp.sum(source * source))
    return lax.fori_loop(0, ITERS, advance, start)[0]


def local(rhs, coefficient, guess):
    conduct = coefficient
    source = rhs
    field = guess
    levels = []
    fields = []
    for level_index in range(3):
        scale = 0.25**level_index
        if level_index > 0:
            field = jnp.zeros_like(source)
        level = setup(conduct, source, scale)
        field = smooth(field, level)
        levels.append(level)
        fields.append(field)
        source = restrict(defect(field, level))
        conduct = restrict(conduct)
    coarse = jnp.stack([conduct, source])
    partial_grid = lax.all_gather(coarse, "wide", axis=1, tiled=True)
    whole = lax.all_gather(partial_grid, "narrow", axis=2, tiled=True)
    faces, diag = weights(whole[0])
    solved = bottom(whole[1], faces, diag, 0.25**3)
    cells_x, cells_z, cells_y = conduct.shape
    correction = lax.dynamic_slice(
        solved,
        (lax.axis_index("wide") * cells_x, lax.axis_index("narrow") * cells_z, jnp.int32(0)),
        (cells_x, cells_z, cells_y),
    )
    for level_index in (2, 1, 0):
        field = fields[level_index] + prolong(correction)
        field = smooth(field, levels[level_index])
        correction = field
    return (field, defect(field, levels[0]))


def solution(mesh):
    return jax.shard_map(
        local,
        mesh=mesh,
        in_specs=(P("wide", "narrow", None), P("wide", "narrow", None), P("wide", "narrow", None)),
        out_specs=(P("wide", "narrow", None), P("wide", "narrow", None)),
        check_vma=False,
    )
```

profile of v0, /device:TPU:9, one launch (start us, length us, event | category | flops | bytes accessed | tf_op | source)
XLA Modules:
  0.0 957.4 jit_solution(17064656083306085985)
XLA Ops:
  10.6 3.9 collective-permute-start.5
  16.4 5.0 collective-permute-start.6
  23.7 3.6 collective-permute-start.2
  39.2 4.3 divide_select_fusion.7
  43.9 4.5 collective-permute-start.8
  50.6 17.0 %collective-permute-done.8 = f32[1,8,128]{0,1,2:T(8,128)S(1)} collective-permute-done((f32[1,8,128]{0,1,2:T(8,128)S(1)}, f32[1,8,128]{0,1,2:T(8,128)S(1)}, u32[]{:S(2)}, u32[]{:S(2)}) %collective-permute-start.8) | collective-permute-done | bytes 4128 | tf_op jit(solution)/shard_map/ppermute | solution.py:14
  68.8 3.5 collective-permute-start.10
  74.3 3.7 collective-permute-start.28
  82.7 6.1 divide_select_fusion.6
  98.9 17.5 %collective-permute-done.12 = f32[1,8,128]{0,1,2:T(8,128)} collective-permute-done((f32[1,8,128]{0,1,2:T(8,128)}, f32[1,8,128]{0,1,2:T(8,128)}, u32[]{:S(2)}, u32[]{:S(2)}) %collective-permute-start.12) | collective-permute-done | bytes 4128 | tf_op jit(solution)/shard_map/ppermute | solution.py:14
  136.3 4.3 collective-permute-start.17
  140.9 16.4 %collective-permute-done.16 = f32[1,8,128]{0,1,2:T(8,128)S(1)} collective-permute-done((f32[1,8,128]{0,1,2:T(8,128)S(1)}, f32[1,8,128]{0,1,2:T(8,128)S(1)}, u32[]{:S(2)}, u32[]{:S(2)}) %collective-permute-start.16) | collective-permute-done | bytes 4128 | tf_op jit(solution)/shard_map/ppermute | solution.py:14
  175.8 4.3 collective-permute-start.21
  180.2 5.6 reshape.236
  189.7 7.6 collective-permute-done.20
  218.2 5.6 reshape.237
  228.3 4.3 collective-permute-start.25
  237.0 3.6 collective-permute-start.26
  257.6 4.3 collective-permute-start.33
  264.5 4.1 collective-permute-start.53
  287.5 4.3 collective-permute-start.37
  308.6 4.4 collective-permute-start.40
  336.7 3.6 collective-permute-start.45
  345.5 3.9 collective-permute-start.46
  360.1 3.9 collective-permute-start.48
  370.9 3.6 collective-permute-start.50
  397.7 3.8 collective-permute-start.60
  416.8 3.6 collective-permute-start.65
  433.8 3.9 collective-permute-start.69
  456.8 19.9 %all_gather.6 = f32[2,16,1,16]{3,0,2,1:T(2,128)S(1)} all-gather(f32[2,2,1,16]{3,0,2,1:T(2,128)S(1)} %copy.236), channel_id=1, replica_groups=mesh['wide'=8,'narrow'=4] {'wide'}, dimensions={1}, use_global_device_ids=true | all-gather | bytes 2304 | tf_op jit(solution)/shard_map/all_gather | solution.py:135
  476.7 8.8 all_gather.7
  487.0 112.1 %while.19 = (s32[]{:T(128)}, f32[16,4,16]{2,1,0:T(4,128)}, f32[16,4,16]{2,1,0:T(4,128)S(1)}, f32[16,4,16]{2,1,0:T(4,128)S(1)}, f32[]{:T(128)}, /*index=5*/f32[16...) while((s32[]{:T(128)}, f32[16,4,16]{2,1,0:T(4,128)}, ...), condition=%wide.region_12.13_spmd.clone, body=%wide.region_9.12_spmd.clone.sunk | while | flops 25604 | bytes 69847 | solution.py:115
  602.5 4.3 collective-permute-start.73
  607.5 4.6 collective-permute-start.74
  618.0 3.6 collective-permute-start.76
  637.7 3.6 collective-permute-start.81
  696.2 3.6 collective-permute-start.93
  718.4 3.7 collective-permute-start.97
  765.2 3.5 collective-permute-start.105
  768.7 18.1 %collective-permute-done.104 = f32[1,8,128]{0,1,2:T(8,128)S(1)} collective-permute-done((f32[1,8,128]{0,1,2:T(8,128)S(1)}, f32[1,8,128]{0,1,2:T(8,128)S(1)}, u32[]{:S(2)}, u32[]{:S(2)}) %collective-permute-start.104) | collective-permute-done | bytes 4128 | tf_op jit(solution)/shard_map/ppermute | solution.py:14
  803.0 4.3 collective-permute-start.109
  807.5 16.7 %collective-permute-done.108 = f32[1,8,128]{0,1,2:T(8,128)S(1)} collective-permute-done((f32[1,8,128]{0,1,2:T(8,128)S(1)}, f32[1,8,128]{0,1,2:T(8,128)S(1)}, u32[]{:S(2)}, u32[]{:S(2)}) %collective-permute-start.108) | collective-permute-done | bytes 4128 | tf_op jit(solution)/shard_map/ppermute | solution.py:14
  841.2 4.3 collective-permute-start.113
  845.7 16.7 %collective-permute-done.112 = f32[1,8,128]{0,1,2:T(8,128)S(1)} collective-permute-done((f32[1,8,128]{0,1,2:T(8,128)S(1)}, f32[1,8,128]{0,1,2:T(8,128)S(1)}, u32[]{:S(2)}, u32[]{:S(2)}) %collective-permute-start.112) | collective-permute-done | bytes 4128 | tf_op jit(solution)/shard_map/ppermute | solution.py:14
  879.3 4.3 collective-permute-start.117
  883.7 16.7 %collective-permute-done.116 = f32[1,8,128]{0,1,2:T(8,128)S(1)} collective-permute-done((f32[1,8,128]{0,1,2:T(8,128)S(1)}, f32[1,8,128]{0,1,2:T(8,128)S(1)}, u32[]{:S(2)}, u32[]{:S(2)}) %collective-permute-start.116) | collective-permute-done | bytes 4128 | tf_op jit(solution)/shard_map/ppermute | solution.py:14
  917.3 4.3 collective-permute-start.121
  921.8 16.7 %collective-permute-done.120 = f32[1,8,128]{0,1,2:T(8,128)S(1)} collective-permute-done((f32[1,8,128]{0,1,2:T(8,128)S(1)}, f32[1,8,128]{0,1,2:T(8,128)S(1)}, u32[]{:S(2)}, u32[]{:S(2)}) %collective-permute-start.120) | collective-permute-done | bytes 4128 | tf_op jit(solution)/shard_map/ppermute | solution.py:14
  (697 shorter events, 591.4 us)
Async XLA Ops:
  1.4 22.0 %collective-permute-start = (f32[2,2,8,128]{3,2,1,0:T(8,128)S(1)}, f32[2,2,8,128]{3,2,1,0:T(8,128)S(1)}, u32[]{:S(2)}, u32[]{:S(2)}) collective-permute-start(f32[2,2,8,128]{3,2,1,0:T(8,128)S(1)} %get-tuple-element.393), channel_id=1, source_target_pairs={{0,4},{4,8},{8,12},{12,16},{16,20},{20,24},{24,28},{1,5},{5,9},{9,... | collective-permute-start | bytes 49160 | tf_op jit(solution)/shard_map/ppermute | solution.py:14
  4.6 18.9 %collective-permute-start.1 = (f32[2,2,8,128]{3,2,1,0:T(8,128)S(1)}, f32[2,2,8,128]{3,2,1,0:T(8,128)S(1)}, u32[]{:S(2)}, u32[]{:S(2)}) collective-permute-start(f32[2,2,8,128]{3,2,1,0:T(8,128)S(1)} %get-tuple-element.394), channel_id=1, source_target_pairs={{4,0},{8,4},{12,8},{16,12},{20,16},{24,20},{28,24},{5,1},{9,5},{13... | collective-permute-start | bytes 49160 | tf_op jit(solution)/shard_map/ppermute | solution.py:17
  8.3 7.6 collective-permute-start.4
  16.4 13.1 %collective-permute-start.6 = (f32[18,1,128]{0,1,2:T(1,128)S(1)}, f32[18,1,128]{0,1,2:T(1,128)S(1)}, u32[]{:S(2)}, u32[]{:S(2)}) collective-permute-start(f32[18,1,128]{0,1,2:T(1,128)S(1)} %copy.206), channel_id=1, source_target_pairs={{0,1},{1,2},{2,3},{4,5},{5,6},{6,7},{8,9},{9,10},{10,11},{12,13},{... | collective-permute-start | bytes 27656 | tf_op jit(solution)/shard_map/ppermute | solution.py:14
  21.5 8.0 collective-permute-start.7
  27.5 7.8 collective-permute-start.3
  43.9 23.7 %collective-permute-start.8 = (f32[1,8,128]{0,1,2:T(8,128)S(1)}, f32[1,8,128]{0,1,2:T(8,128)S(1)}, u32[]{:S(2)}, u32[]{:S(2)}) collective-permute-start(f32[1,8,128]{0,1,2:T(8,128)S(1)} %get-tuple-element.344), channel_id=1, source_target_pairs={{0,4},{4,8},{8,12},{12,16},{16,20},{20,24},{24,28},{1,5},{5,9},{9,... | collective-permute-start | bytes 12296 | tf_op jit(solution)/shard_map/ppermute | solution.py:14
  48.4 19.6 %collective-permute-start.9 = (f32[1,8,128]{0,1,2:T(8,128)S(1)}, f32[1,8,128]{0,1,2:T(8,128)S(1)}, u32[]{:S(2)}, u32[]{:S(2)}) collective-permute-start(f32[1,8,128]{0,1,2:T(8,128)S(1)} %get-tuple-element.345), channel_id=1, source_target_pairs={{4,0},{8,4},{12,8},{16,12},{20,16},{24,20},{28,24},{5,1},{9,5},{13... | collective-permute-start | bytes 12296 | tf_op jit(solution)/shard_map/ppermute | solution.py:17
  68.8 11.7 %collective-permute-start.10 = (f32[18,1,128]{0,1,2:T(1,128)S(1)}, f32[18,1,128]{0,1,2:T(1,128)S(1)}, u32[]{:S(2)}, u32[]{:S(2)}) collective-permute-start(f32[18,1,128]{0,1,2:T(1,128)S(1)} %get-tuple-element.314), channel_id=1, source_target_pairs={{0,1},{1,2},{2,3},{4,5},{5,6},{6,7},{8,9},{9,10},{10,11},{12,13},{... | collective-permute-start | bytes 27656 | tf_op jit(solution)/shard_map/ppermute | solution.py:14
  72.4 8.2 collective-permute-start.11
  74.3 158.2 %collective-permute-start.28 = (f32[1,4,64]{2,1,0:T(4,128)S(1)}, f32[1,4,64]{2,1,0:T(4,128)S(1)}, u32[]{:S(2)}, u32[]{:S(2)}) collective-permute-start(f32[1,4,64]{2,1,0:T(4,128)S(1)} %broadcast.359), channel_id=1, source_target_pairs={{0,4},{4,8},{8,12},{12,16},{16,20},{20,24},{24,28},{1,5},{5,9},{9,... | collective-permute-start | bytes 3080 | tf_op jit(solution)/shard_map/ppermute | solution.py:14
  78.0 154.6 %collective-permute-start.29 = (f32[1,4,64]{2,1,0:T(4,128)S(1)}, f32[1,4,64]{2,1,0:T(4,128)S(1)}, u32[]{:S(2)}, u32[]{:S(2)}) collective-permute-start(f32[1,4,64]{2,1,0:T(4,128)S(1)} %broadcast.359), channel_id=1, source_target_pairs={{4,0},{8,4},{12,8},{16,12},{20,16},{24,20},{28,24},{5,1},{9,5},{13... | collective-permute-start | bytes 3080 | tf_op jit(solution)/shard_map/ppermute | solution.py:17
  91.1 25.2 %collective-permute-start.12 = (f32[1,8,128]{0,1,2:T(8,128)}, f32[1,8,128]{0,1,2:T(8,128)}, u32[]{:S(2)}, u32[]{:S(2)}) collective-permute-start(f32[1,8,128]{0,1,2:T(8,128)} %get-tuple-element.342), channel_id=1, source_target_pairs={{0,4},{4,8},{8,12},{12,16},{16,20},{20,24},{24,28},{1,5},{5,9},{9,... | collective-permute-start | bytes 12296 | tf_op jit(solution)/shard_map/ppermute | solution.py:14
  93.9 24.7 %collective-permute-start.13 = (f32[1,8,128]{0,1,2:T(8,128)}, f32[1,8,128]{0,1,2:T(8,128)}, u32[]{:S(2)}, u32[]{:S(2)}) collective-permute-start(f32[1,8,128]{0,1,2:T(8,128)} %get-tuple-element.343), channel_id=1, source_target_pairs={{4,0},{8,4},{12,8},{16,12},{20,16},{24,20},{28,24},{5,1},{9,5},{13... | collective-permute-start | bytes 12296 | tf_op jit(solution)/shard_map/ppermute | solution.py:17
  134.4 22.9 %collective-permute-start.16 = (f32[1,8,128]{0,1,2:T(8,128)S(1)}, f32[1,8,128]{0,1,2:T(8,128)S(1)}, u32[]{:S(2)}, u32[]{:S(2)}) collective-permute-start(f32[1,8,128]{0,1,2:T(8,128)S(1)} %get-tuple-element.340), channel_id=1, source_target_pairs={{0,4},{4,8},{8,12},{12,16},{16,20},{20,24},{24,28},{1,5},{5,9},{9,... | collective-permute-start | bytes 12296 | tf_op jit(solution)/shard_map/ppermute | solution.py:14
  136.3 24.0 %collective-permute-start.17 = (f32[1,8,128]{0,1,2:T(8,128)S(1)}, f32[1,8,128]{0,1,2:T(8,128)S(1)}, u32[]{:S(2)}, u32[]{:S(2)}) collective-permute-start(f32[1,8,128]{0,1,2:T(8,128)S(1)} %get-tuple-element.341), channel_id=1, source_target_pairs={{4,0},{8,4},{12,8},{16,12},{20,16},{24,20},{28,24},{5,1},{9,5},{13... | collective-permute-start | bytes 12296 | tf_op jit(solution)/shard_map/ppermute | solution.py:17
  173.9 23.4 %collective-permute-start.20 = (f32[1,8,128]{0,1,2:T(8,128)}, f32[1,8,128]{0,1,2:T(8,128)}, u32[]{:S(2)}, u32[]{:S(2)}) collective-permute-start(f32[1,8,128]{0,1,2:T(8,128)} %get-tuple-element.338), channel_id=1, source_target_pairs={{0,4},{4,8},{8,12},{12,16},{16,20},{20,24},{24,28},{1,5},{5,9},{9,... | collective-permute-start | bytes 12296 | tf_op jit(solution)/shard_map/ppermute | solution.py:14
  175.8 24.8 %collective-permute-start.21 = (f32[1,8,128]{0,1,2:T(8,128)}, f32[1,8,128]{0,1,2:T(8,128)}, u32[]{:S(2)}, u32[]{:S(2)}) collective-permute-start(f32[1,8,128]{0,1,2:T(8,128)} %get-tuple-element.339), channel_id=1, source_target_pairs={{4,0},{8,4},{12,8},{16,12},{20,16},{24,20},{28,24},{5,1},{9,5},{13... | collective-permute-start | bytes 12296 | tf_op jit(solution)/shard_map/ppermute | solution.py:17
  226.4 10.6 %collective-permute-start.24 = (f32[2,2,4,64]{3,2,1,0:T(4,128)S(1)}, f32[2,2,4,64]{3,2,1,0:T(4,128)S(1)}, u32[]{:S(2)}, u32[]{:S(2)}) collective-permute-start(f32[2,2,4,64]{3,2,1,0:T(4,128)S(1)} %get-tuple-element.407), channel_id=1, source_target_pairs={{0,4},{4,8},{8,12},{12,16},{16,20},{20,24},{24,28},{1,5},{5,9},{9,... | collective-permute-start | bytes 12296 | tf_op jit(solution)/shard_map/ppermute | solution.py:14
  228.3 8.7 collective-permute-start.25
  232.6 10.0 %collective-permute-start.30 = (f32[10,1,64]{2,1,0:T(1,128)S(1)}, f32[10,1,64]{2,1,0:T(1,128)S(1)}, u32[]{:S(2)}, u32[]{:S(2)}) collective-permute-start(f32[10,1,64]{2,1,0:T(1,128)S(1)} %get-tuple-element.437), channel_id=1, source_target_pairs={{0,1},{1,2},{2,3},{4,5},{5,6},{6,7},{8,9},{9,10},{10,11},{12,13},{... | collective-permute-start | bytes 7688 | tf_op jit(solution)/shard_map/ppermute | solution.py:14
  235.0 7.6 collective-permute-start.31
  255.7 15.6 %collective-permute-start.32 = (f32[1,4,64]{0,2,1:T(8,128)}, f32[1,4,64]{0,2,1:T(8,128)}, u32[]{:S(2)}, u32[]{:S(2)}) collective-permute-start(f32[1,4,64]{0,2,1:T(8,128)} %get-tuple-element.387), channel_id=1, source_target_pairs={{0,4},{4,8},{8,12},{12,16},{16,20},{20,24},{24,28},{1,5},{5,9},{9,... | collective-permute-start | bytes 3080 | tf_op jit(solution)/shard_map/ppermute | solution.py:14
  257.6 14.7 %collective-permute-start.33 = (f32[1,4,64]{0,2,1:T(8,128)}, f32[1,4,64]{0,2,1:T(8,128)}, u32[]{:S(2)}, u32[]{:S(2)}) collective-permute-start(f32[1,4,64]{0,2,1:T(8,128)} %get-tuple-element.388), channel_id=1, source_target_pairs={{4,0},{8,4},{12,8},{16,12},{20,16},{24,20},{28,24},{5,1},{9,5},{13... | collective-permute-start | bytes 3080 | tf_op jit(solution)/shard_map/ppermute | solution.py:17
  262.5 88.8 %collective-permute-start.52 = (f32[1,2,32]{2,0,1:T(1,128)}, f32[1,2,32]{2,0,1:T(1,128)}, u32[]{:S(2)}, u32[]{:S(2)}) collective-permute-start(f32[1,2,32]{2,0,1:T(1,128)} %broadcast.368), channel_id=1, source_target_pairs={{0,4},{4,8},{8,12},{12,16},{16,20},{20,24},{24,28},{1,5},{5,9},{9,... | collective-permute-start | bytes 776 | tf_op jit(solution)/shard_map/ppermute | solution.py:14
  264.5 86.8 %collective-permute-start.53 = (f32[1,2,32]{2,0,1:T(1,128)}, f32[1,2,32]{2,0,1:T(1,128)}, u32[]{:S(2)}, u32[]{:S(2)}) collective-permute-start(f32[1,2,32]{2,0,1:T(1,128)} %broadcast.368), channel_id=1, source_target_pairs={{4,0},{8,4},{12,8},{16,12},{20,16},{24,20},{28,24},{5,1},{9,5},{13... | collective-permute-start | bytes 776 | tf_op jit(solution)/shard_map/ppermute | solution.py:17
  285.6 8.5 collective-permute-start.36
  287.5 7.8 collective-permute-start.37
  308.6 8.8 collective-permute-start.40
  320.9 8.2 collective-permute-start.42
  333.9 7.7 collective-permute-start.44
  336.7 7.7 collective-permute-start.45
  360.1 10.7 %collective-permute-start.48 = (f32[2,2,2,32]{3,1,2,0:T(2,128)S(1)}, f32[2,2,2,32]{3,1,2,0:T(2,128)S(1)}, u32[]{:S(2)}, u32[]{:S(2)}) collective-permute-start(f32[2,2,2,32]{3,1,2,0:T(2,128)S(1)} %get-tuple-element.479), channel_id=1, source_target_pairs={{0,4},{4,8},{8,12},{12,16},{16,20},{20,24},{24,28},{1,5},{5,9},{9,... | collective-permute-start | bytes 3080 | tf_op jit(solution)/shard_map/ppermute | solution.py:14
  366.4 10.1 %collective-permute-start.54 = (f32[6,1,32]{2,0,1:T(8,128)S(1)}, f32[6,1,32]{2,0,1:T(8,128)S(1)}, u32[]{:S(2)}, u32[]{:S(2)}) collective-permute-start(f32[6,1,32]{2,0,1:T(8,128)S(1)} %get-tuple-element.481), channel_id=1, source_target_pairs={{0,1},{1,2},{2,3},{4,5},{5,6},{6,7},{8,9},{9,10},{10,11},{12,13},{... | collective-permute-start | bytes 2312 | tf_op jit(solution)/shard_map/ppermute | solution.py:14
  431.3 10.0 %collective-permute-start.68 = (f32[1,2,32]{2,0,1:T(1,128)}, f32[1,2,32]{2,0,1:T(1,128)}, u32[]{:S(2)}, u32[]{:S(2)}) collective-permute-start(f32[1,2,32]{2,0,1:T(1,128)} %get-tuple-element.453), channel_id=1, source_target_pairs={{0,4},{4,8},{8,12},{12,16},{16,20},{20,24},{24,28},{1,5},{5,9},{9,... | collective-permute-start | bytes 776 | tf_op jit(solution)/shard_map/ppermute | solution.py:14
  693.7 7.9 collective-permute-start.92
  715.7 8.2 collective-permute-start.96
  738.6 8.0 collective-permute-start.100
  762.1 24.6 %collective-permute-start.104 = (f32[1,8,128]{0,1,2:T(8,128)S(1)}, f32[1,8,128]{0,1,2:T(8,128)S(1)}, u32[]{:S(2)}, u32[]{:S(2)}) collective-permute-start(f32[1,8,128]{0,1,2:T(8,128)S(1)} %get-tuple-element.353), channel_id=1, source_target_pairs={{0,4},{4,8},{8,12},{12,16},{16,20},{20,24},{24,28},{1,5},{5,9},{9,... | collective-permute-start | bytes 12296 | tf_op jit(solution)/shard_map/ppermute | solution.py:14
  765.2 23.9 %collective-permute-start.105 = (f32[1,8,128]{0,1,2:T(8,128)S(1)}, f32[1,8,128]{0,1,2:T(8,128)S(1)}, u32[]{:S(2)}, u32[]{:S(2)}) collective-permute-start(f32[1,8,128]{0,1,2:T(8,128)S(1)} %get-tuple-element.354), channel_id=1, source_target_pairs={{4,0},{8,4},{12,8},{16,12},{20,16},{24,20},{28,24},{5,1},{9,5},{13... | collective-permute-start | bytes 12296 | tf_op jit(solution)/shard_map/ppermute | solution.py:17
  801.1 23.1 %collective-permute-start.108 = (f32[1,8,128]{0,1,2:T(8,128)S(1)}, f32[1,8,128]{0,1,2:T(8,128)S(1)}, u32[]{:S(2)}, u32[]{:S(2)}) collective-permute-start(f32[1,8,128]{0,1,2:T(8,128)S(1)} %get-tuple-element.327), channel_id=1, source_target_pairs={{0,4},{4,8},{8,12},{12,16},{16,20},{20,24},{24,28},{1,5},{5,9},{9,... | collective-permute-start | bytes 12296 | tf_op jit(solution)/shard_map/ppermute | solution.py:14
  803.0 24.5 %collective-permute-start.109 = (f32[1,8,128]{0,1,2:T(8,128)S(1)}, f32[1,8,128]{0,1,2:T(8,128)S(1)}, u32[]{:S(2)}, u32[]{:S(2)}) collective-permute-start(f32[1,8,128]{0,1,2:T(8,128)S(1)} %get-tuple-element.328), channel_id=1, source_target_pairs={{4,0},{8,4},{12,8},{16,12},{20,16},{24,20},{28,24},{5,1},{9,5},{13... | collective-permute-start | bytes 12296 | tf_op jit(solution)/shard_map/ppermute | solution.py:17
  839.3 23.1 %collective-permute-start.112 = (f32[1,8,128]{0,1,2:T(8,128)S(1)}, f32[1,8,128]{0,1,2:T(8,128)S(1)}, u32[]{:S(2)}, u32[]{:S(2)}) collective-permute-start(f32[1,8,128]{0,1,2:T(8,128)S(1)} %get-tuple-element.325), channel_id=1, source_target_pairs={{0,4},{4,8},{8,12},{12,16},{16,20},{20,24},{24,28},{1,5},{5,9},{9,... | collective-permute-start | bytes 12296 | tf_op jit(solution)/shard_map/ppermute | solution.py:14
  841.2 24.5 %collective-permute-start.113 = (f32[1,8,128]{0,1,2:T(8,128)S(1)}, f32[1,8,128]{0,1,2:T(8,128)S(1)}, u32[]{:S(2)}, u32[]{:S(2)}) collective-permute-start(f32[1,8,128]{0,1,2:T(8,128)S(1)} %get-tuple-element.326), channel_id=1, source_target_pairs={{4,0},{8,4},{12,8},{16,12},{20,16},{24,20},{28,24},{5,1},{9,5},{13... | collective-permute-start | bytes 12296 | tf_op jit(solution)/shard_map/ppermute | solution.py:17
  877.3 23.1 %collective-permute-start.116 = (f32[1,8,128]{0,1,2:T(8,128)S(1)}, f32[1,8,128]{0,1,2:T(8,128)S(1)}, u32[]{:S(2)}, u32[]{:S(2)}) collective-permute-start(f32[1,8,128]{0,1,2:T(8,128)S(1)} %get-tuple-element.323), channel_id=1, source_target_pairs={{0,4},{4,8},{8,12},{12,16},{16,20},{20,24},{24,28},{1,5},{5,9},{9,... | collective-permute-start | bytes 12296 | tf_op jit(solution)/shard_map/ppermute | solution.py:14
  879.3 24.5 %collective-permute-start.117 = (f32[1,8,128]{0,1,2:T(8,128)S(1)}, f32[1,8,128]{0,1,2:T(8,128)S(1)}, u32[]{:S(2)}, u32[]{:S(2)}) collective-permute-start(f32[1,8,128]{0,1,2:T(8,128)S(1)} %get-tuple-element.324), channel_id=1, source_target_pairs={{4,0},{8,4},{12,8},{16,12},{20,16},{24,20},{28,24},{5,1},{9,5},{13... | collective-permute-start | bytes 12296 | tf_op jit(solution)/shard_map/ppermute | solution.py:17
  915.4 23.1 %collective-permute-start.120 = (f32[1,8,128]{0,1,2:T(8,128)S(1)}, f32[1,8,128]{0,1,2:T(8,128)S(1)}, u32[]{:S(2)}, u32[]{:S(2)}) collective-permute-start(f32[1,8,128]{0,1,2:T(8,128)S(1)} %get-tuple-element.321), channel_id=1, source_target_pairs={{0,4},{4,8},{8,12},{12,16},{16,20},{20,24},{24,28},{1,5},{5,9},{9,... | collective-permute-start | bytes 12296 | tf_op jit(solution)/shard_map/ppermute | solution.py:14
  917.3 24.5 %collective-permute-start.121 = (f32[1,8,128]{0,1,2:T(8,128)S(1)}, f32[1,8,128]{0,1,2:T(8,128)S(1)}, u32[]{:S(2)}, u32[]{:S(2)}) collective-permute-start(f32[1,8,128]{0,1,2:T(8,128)S(1)} %get-tuple-element.322), channel_id=1, source_target_pairs={{4,0},{8,4},{12,8},{16,12},{20,16},{24,20},{28,24},{5,1},{9,5},{13... | collective-permute-start | bytes 12296 | tf_op jit(solution)/shard_map/ppermute | solution.py:17
  (157 other events, 1812.2 us)
where the time goes:
time: 974 us; the launch traced here: 957 us
  starting transfers between devices  350 us (36%)
  waiting for transfers between devices  254 us (26%)
  other arithmetic  194 us (20%)
  local copies, waits for them, and re-layouts  86.9 us (9%)
  loops' own time  39.7 us (4%)
  blocking collectives  28.7 us (3%)
    ppermute x62, starting transfers between devices, padded_2(): lax.ppermute(lax.slice_in_dim(block, 0, width, axis=dim), axis, backward)  175 us
    ppermute x62, starting transfers between devices, padded_2(): lax.ppermute(lax.slice_in_dim(block, block.shape[dim] - width, None, axis...  174 us
    ppermute x62, waiting for transfers between devices, padded_2(): lax.ppermute(lax.slice_in_dim(block, block.shape[dim] - width, None, axis...  144 us
    ppermute x62, waiting for transfers between devices, padded_2(): lax.ppermute(lax.slice_in_dim(block, 0, width, axis=dim), axis, backward)  109 us
    select_n x24, other arithmetic, smooth(): field = trimmed(jnp.where(inner_colour == parity, fresh, wider))  51.3 us
    another operation x1, loops' own time, bottom(): return lax.fori_loop(0, ITERS, advance, start)[0]  39.7 us
    reduce_sum x20, other arithmetic, advance(): alpha = norm_now / jnp.sum(search * image)  31.3 us
    add x20, other arithmetic, advance(): search = remain + norm_next / norm_now * search  27.1 us
  transfers between devices with their start and end apart: 124, of which 59 were waited for; matrix products, arithmetic and copies ran while one was open for 12% of the time, Pallas kernels for 0%

commit v1 on v0

v1 whole, which is shorter than its diff:
```python
import functools

import jax
import jax.numpy as jnp
from jax import lax
from jax.experimental import pallas as pl
from jax.experimental.pallas import tpu as pltpu
from jax.sharding import PartitionSpec as P

ITERS = 20
LANES = 128
DEEP = 5
SIDE = 8
PAD = 2
MESH = pl.DeviceIdType.MESH


def dot(a, b):
    return lax.dot_general(
        a, b, (((1,), (0,)), ((), ())), precision=lax.Precision.HIGHEST, preferred_element_type=jnp.float32
    )


def iota(shape, dim):
    return lax.broadcasted_iota(jnp.int32, shape, dim)


def one(cond):
    return jnp.where(cond, 1.0, 0.0).astype(jnp.float32)


def coarse_lane(lane, part, ny):
    shift = ny.bit_length() - 1
    z = part * (LANES // ny) + (lane >> shift)
    return (z >> 1) * (ny // 2) + ((lane & (ny - 1)) >> 1)


def down_lanes(part, ny):
    shape = (LANES, LANES)
    return one(iota(shape, 1) == coarse_lane(iota(shape, 0), part, ny))


def up_lanes(part, ny):
    shape = (LANES, LANES)
    return one(iota(shape, 0) == coarse_lane(iota(shape, 1), part, ny))


def down_rows(rows):
    shape = (rows // 2, rows)
    return one(iota(shape, 0) == (iota(shape, 1) >> 1))


def up_rows(rows, coarse, first):
    shape = (rows, coarse)
    return one(iota(shape, 1) == (iota(shape, 0) >> 1) + first)


class Level:
    def __init__(self, k, f, u, wx, wy, wzp, wzm, diag, inv, ny, first, last, off=0, odd=0):
        self.k, self.f, self.u = k, f, u
        self.wx, self.wy, self.wzp, self.wzm, self.diag, self.inv = wx, wy, wzp, wzm, diag, inv
        self.ny, self.first, self.last, self.off, self.odd = ny, first, last, off, odd
        self.rows = k.shape[1]
        self.tiles = k.shape[0]

    def above(self, here, after):
        if self.ny == LANES:
            return after
        lane = iota(here.shape, 1)
        step = LANES - self.ny
        return jnp.where(lane < step, pltpu.roll(here, step, 1), pltpu.roll(after, step, 1))

    def below(self, here, before):
        if self.ny == LANES:
            return before
        lane = iota(here.shape, 1)
        return jnp.where(lane >= self.ny, pltpu.roll(here, self.ny, 1), pltpu.roll(before, self.ny, 1))

    def operator(self):
        shape = (self.rows, LANES)
        row = iota(shape, 0)
        y = iota(shape, 1) & (self.ny - 1)
        zero = jnp.zeros(shape, jnp.float32)
        for t in range(self.first, self.last):
            k = self.k[t]
            after = self.k[t + 1] if t + 1 < self.tiles else zero
            before = self.k[t - 1] if t > 0 else zero
            xp = jnp.where(row == self.rows - 1, 0.0, pltpu.roll(k, self.rows - 1, 0))
            xm = jnp.where(row == 0, 0.0, pltpu.roll(k, 1, 0))
            yp = jnp.where(y == self.ny - 1, 0.0, pltpu.roll(k, LANES - 1, 1))
            ym = jnp.where(y == 0, 0.0, pltpu.roll(k, 1, 1))
            zp = self.above(k, after)
            zm = self.below(k, before)
            diag = 3.0 * k + 0.5 * (xp + xm + zp + zm + yp + ym)
            diag = jnp.where(diag > 0.0, diag, 1.0)
            live = k > 0.0

            def face(other):
                return jnp.where(live & (other > 0.0), 0.5 * (k + other), 0.0)

            self.wx[t] = face(xp)
            self.wy[t] = face(yp)
            self.wzp[t] = face(zp)
            self.wzm[t] = face(zm)
            self.diag[t] = diag
            self.inv[t] = 1.0 / diag

    def beside(self, t, here, after, before):
        wx = self.wx[t]
        wy = self.wy[t]
        total = wx * pltpu.roll(here, self.rows - 1, 0) + pltpu.roll(wx * here, 1, 0)
        total = total + (wy * pltpu.roll(here, LANES - 1, 1) + pltpu.roll(wy * here, 1, 1))
        return total + (self.wzp[t] * self.above(here, after) + self.wzm[t] * self.below(here, before))

    def around(self, t):
        here = self.u[t + self.off]
        after = self.u[t + 1 + self.off] if t + 1 < self.tiles else here
        before = self.u[t - 1 + self.off] if t > 0 else here
        return here, after, before

    def smooth(self):
        shape = (self.rows, LANES)
        shift = self.ny.bit_length() - 1
        lane = iota(shape, 1)
        place = iota(shape, 0) + (lane >> shift) + (lane & (self.ny - 1)) + self.odd

        @pl.loop(0, 4)
        def _(step):
            even = ((place + step) & 1) == 0
            other = ((place + step) & 1) == 1
            for t in range(self.first, self.last):
                here, after, before = self.around(t)
                fresh = (self.f[t] + self.beside(t, here, after, before)) * self.inv[t]
                mask = other if (self.ny == LANES and t % 2 == 1) else even
                self.u[t + self.off] = jnp.where(mask, fresh, here)

    def defect(self, t):
        here, after, before = self.around(t)
        return self.f[t] - (self.diag[t] * here - self.beside(t, here, after, before))


def kernel(wide, narrow, rhs, cond, guess, pressure, residual, *scratch):
    (p0, u0r, op0, a1, u1r, u1, op1, a2, own2, g2, u2, op2, a3, op3,
     send0, recv0, send1, recv1, send2, recv2) = scratch
    w = lax.axis_index("wide")
    n = lax.axis_index("narrow")
    bx, bz, _ = rhs.shape
    hx, hz = bx // 2, bz // 2
    own_z = pl.ds(DEEP, bz)
    own_x = pl.ds(SIDE, bx)
    tiles_own = hz // 2
    f32 = jnp.float32

    for ref in (p0, u0r, a1, u1r):
        ref[...] = jnp.zeros(ref.shape, f32)
    u1[...] = jnp.zeros(u1.shape, f32)

    def valid(dw):
        return (w + dw >= 0) & (w + dw < wide)

    def when(cond_, body):
        if cond_ is True:
            body()
        else:
            pl.when(cond_)(body)

    barrier = pltpu.get_barrier_semaphore()

    def greet(dev):
        pl.semaphore_signal(barrier, inc=1, device_id=dev, device_id_type=MESH)

    for j in range(1, narrow):
        greet((w, lax.rem(n + j, narrow)))
    for dw in (-1, 1):
        @pl.when(valid(dw))
        def _(dw=dw):
            for j in range(narrow):
                greet((w + dw, lax.rem(n + j, narrow)))

    @pl.loop(0, wide)
    def _(other):
        @pl.when((other < w - 1) | (other > w + 1))
        def _():
            greet((other, n))

    for z in range(bz):
        p0[0, DEEP + z, SIDE:SIDE + bx, :] = cond[:, z, :]
        p0[1, DEEP + z, SIDE:SIDE + bx, :] = rhs[:, z, :]
        p0[2, DEEP + z, SIDE:SIDE + bx, :] = guess[:, z, :]

    half = down_rows(bx)
    lanes0 = [down_lanes(i, LANES) for i in (0, 2)]

    def to_level_1(index, slices, factor):
        for tt in range(tiles_own):
            four = [slices[4 * tt + i] for i in range(4)]
            spread = dot(four[0] + four[1], lanes0[0]) + dot(four[2] + four[3], lanes0[1])
            a1[index, n * tiles_own + tt, SIDE:SIDE + hx, :] = factor * dot(half, spread)

    to_level_1(0, [p0[0, DEEP + z, SIDE:SIDE + bx, :] for z in range(bz)], 0.125)

    near = jnp.where(w > 0, 1, 0) + jnp.where(w < wide - 1, 1, 0)
    pl.semaphore_wait(barrier, (wide - 1 - near) + near * narrow + narrow - 1)

    zs = {1: (DEEP + bz - DEEP, 0, DEEP), -1: (DEEP, DEEP + bz, DEEP), 0: (DEEP, DEEP, bz)}
    xs = {1: (SIDE + bx - SIDE, 0, SIDE), -1: (SIDE, SIDE + bx, SIDE), 0: (SIDE, SIDE, bx)}
    around = [(dw, dn) for dw in (-1, 0, 1) for dn in (-1, 0, 1) if (dw, dn) != (0, 0)]

    def has(dw, dn):
        good = None
        if dw:
            good = valid(dw)
        if dn:
            zgood = (n + dn >= 0) & (n + dn < narrow)
            good = zgood if good is None else good & zgood
        return good

    def fine(which, dw, dn):
        src_z, dst_z, len_z = zs[dn]
        src_x, dst_x, len_x = xs[dw]
        ref = p0 if which == 0 else u0r
        lead = (slice(None),) if which == 0 else ()
        src = ref.at[lead + (pl.ds(src_z, len_z), pl.ds(src_x, len_x))]
        dst = ref.at[lead + (pl.ds(dst_z, len_z), pl.ds(dst_x, len_x))]
        mine = (dw + 1) * 3 + dn + 1
        theirs = (1 - dw) * 3 + 1 - dn
        return pltpu.make_async_remote_copy(
            src_ref=src, dst_ref=dst, send_sem=send0.at[which, mine], recv_sem=recv0.at[which, theirs],
            device_id=(w + dw, n + dn), device_id_type=MESH)

    def fine_in(which, dw, dn):
        _, dst_z, len_z = zs[-dn]
        _, dst_x, len_x = xs[-dw]
        ref = p0 if which == 0 else u0r
        lead = (slice(None),) if which == 0 else ()
        dst = ref.at[lead + (pl.ds(dst_z, len_z), pl.ds(dst_x, len_x))]
        mine = (dw + 1) * 3 + dn + 1
        return pltpu.make_async_remote_copy(
            src_ref=dst, dst_ref=dst, send_sem=send0.at[which, mine], recv_sem=recv0.at[which, mine],
            device_id=(w + dw, n + dn), device_id_type=MESH)

    def fine_start(which):
        for dw, dn in around:
            pl.when(has(dw, dn))(lambda dw=dw, dn=dn: fine(which, dw, dn).start())

    def fine_recv(which):
        for dw, dn in around:
            pl.when(has(dw, dn))(lambda dw=dw, dn=dn: fine_in(which, dw, dn).wait_recv())

    def fine_sent(which):
        for dw, dn in around:
            pl.when(has(dw, dn))(lambda dw=dw, dn=dn: fine(which, dw, dn).wait_send())

    mid = [(dw, j) for dw in (0, -1, 1) for j in range(narrow) if (dw, j) != (0, 0)]

    def mid_ref(which):
        return u1r if which == 2 else a1.at[which]

    def middle(which, dw, j):
        ref = mid_ref(which)
        tile = pl.ds(n * tiles_own, tiles_own)
        return pltpu.make_async_remote_copy(
            src_ref=ref.at[tile, pl.ds(SIDE, hx)], dst_ref=ref.at[tile, pl.ds(SIDE - dw * hx, hx)],
            send_sem=send1.at[which, dw + 1, j], recv_sem=recv1.at[which, 1 - dw, j],
            device_id=(w + dw, lax.rem(n + j, narrow)), device_id_type=MESH)

    def middle_in(which, dw, j):
        ref = mid_ref(which)
        src = lax.rem(n + narrow - j, narrow)
        dst = ref.at[pl.ds(src * tiles_own, tiles_own), pl.ds(SIDE + dw * hx, hx)]
        return pltpu.make_async_remote_copy(
            src_ref=dst, dst_ref=dst, send_sem=send1.at[which, dw + 1, j], recv_sem=recv1.at[which, dw + 1, j],
            device_id=(w + dw, src), device_id_type=MESH)

    def each_mid(fun):
        for dw, j in mid:
            if dw == 0:
                fun(dw, j)
            else:
                pl.when(valid(dw))(lambda dw=dw, j=j: fun(dw, j))

    def mid_start(which):
        each_mid(lambda dw, j: middle(which, dw, j).start())

    def mid_recv(which):
        each_mid(lambda dw, j: middle_in(which, dw, j).wait_recv())

    def mid_sent(which):
        each_mid(lambda dw, j: middle(which, dw, j).wait_send())

    def top(which, step):
        other = lax.rem(w + step, wide)
        return pltpu.make_async_remote_copy(
            src_ref=own2.at[which], dst_ref=g2.at[which, w], send_sem=send2.at[which, step],
            recv_sem=recv2.at[which, step], device_id=(other, n), device_id_type=MESH)

    def top_in(which, step):
        src = lax.rem(w + wide - step, wide)
        return pltpu.make_async_remote_copy(
            src_ref=own2.at[which], dst_ref=g2.at[which, src], send_sem=send2.at[which, step],
            recv_sem=recv2.at[which, step], device_id=(src, n), device_id_type=MESH)

    def each_top(fun):
        @pl.loop(1, wide)
        def _(step):
            fun(step)

    fine_start(0)
    mid_start(0)
    fine_recv(0)

    names = range(6)
    ny = LANES
    zero_level = Level(p0.at[0], p0.at[1], p0.at[2], *[op0.at[i] for i in names], LANES, 1, 2 * DEEP + bz - 1, odd=1)
    zero_level.operator()
    fine_sent(0)
    zero_level.smooth()
    to_level_1(1, [zero_level.defect(DEEP + z)[SIDE:SIDE + bx] for z in range(bz)], 0.5)
    mid_start(1)
    u0r[own_z, own_x, :] = p0[2, own_z, own_x, :]
    fine_start(1)

    ny1, ny2, ny3 = LANES // 2, LANES // 4, LANES // 8
    mid_recv(0)
    one_level = Level(a1.at[0], a1.at[1], u1, *[op1.at[i] for i in names], ny1, 0, a1.shape[1], off=PAD)
    rows2 = hx // 2
    lanes1 = [down_lanes(i, ny1) for i in range(4)]
    tiles2 = a1.shape[1] // 4

    def to_level_2(which, tiles, factor):
        shape = (tiles2 * rows2, hx)
        pack = None
        for big in range(tiles2):
            spread = dot(tiles[4 * big], lanes1[0])
            for i in range(1, 4):
                spread = spread + dot(tiles[4 * big + i], lanes1[i])
            place = one(iota(shape, 0) == (iota(shape, 1) >> 1) + big * rows2)
            part = dot(place, spread)
            pack = part if pack is None else pack + part
        pack = factor * pack
        own2[which] = pack
        g2[which, w] = pack

    to_level_2(0, [a1[0, t, SIDE:SIDE + hx, :] for t in range(a1.shape[1])], 0.125)
    each_top(lambda step: top(0, step).start())
    one_level.operator()
    mid_recv(1)
    one_level.smooth()
    to_level_2(1, [one_level.defect(t)[SIDE:SIDE + hx] for t in range(a1.shape[1])], 0.5)
    each_top(lambda step: top(1, step).start())
    u1r[pl.ds(n * tiles_own, tiles_own), SIDE:SIDE + hx, :] = u1[pl.ds(PAD + n * tiles_own, tiles_own), SIDE:SIDE + hx, :]
    mid_start(2)

    def unpack(which):
        for other in range(wide):
            for t in range(tiles2):
                a2[which, t, other * rows2:(other + 1) * rows2, :] = g2[which, other, t * rows2:(t + 1) * rows2, :]

    each_top(lambda step: top_in(0, step).wait_recv())
    unpack(0)
    two_level = Level(a2.at[0], a2.at[1], u2, *[op2.at[i] for i in names], ny2, 0, tiles2)
    two_level.operator()
    all2, all3 = a2.shape[2], a3.shape[2]
    half2 = down_rows(all2)
    lanes2 = [down_lanes(i, ny2) for i in range(tiles2)]

    def to_level_3(tiles, factor):
        spread = dot(tiles[0], lanes2[0])
        for i in range(1, tiles2):
            spread = spread + dot(tiles[i], lanes2[i])
        return factor * dot(half2, spread)

    a3[0, 0] = to_level_3([a2[0, t] for t in range(tiles2)], 0.125)
    last = Level(a3.at[0], a3.at[1], a3.at[1], *[op3.at[i] for i in names], ny3, 0, 1)
    last.operator()
    each_top(lambda step: top_in(1, step).wait_recv())
    unpack(1)
    u2[...] = jnp.zeros(u2.shape, f32)
    two_level.smooth()
    source = to_level_3([two_level.defect(t) for t in range(tiles2)], 0.5)

    def image(v):
        return last.diag[0] * v - last.beside(0, v, v, v)

    def total(v):
        return jnp.sum(jnp.sum(v, axis=0, keepdims=True), axis=1, keepdims=True)

    first_image = image(source)
    rr = total(source * source)
    alpha = rr / total(source * first_image)

    def advance(step, carry):
        answer, remain, search, moved, norm, alpha = carry
        answer = answer + alpha * search
        remain = remain - alpha * moved
        fresh = image(remain)
        norm_next = total(remain * remain)
        cross = total(remain * fresh)
        beta = norm_next / norm
        alpha_next = norm_next / (cross - beta * norm_next / alpha)
        search = remain + beta * search
        moved = fresh + beta * moved
        return answer, remain, search, moved, norm_next, alpha_next

    carry = (jnp.zeros_like(source), source, source, first_image, rr, alpha)
    carry = lax.fori_loop(0, ITERS - 1, advance, carry)
    solved = carry[0] + carry[5] * carry[2]

    wider = dot(up_rows(all2, all3, 0), solved)
    for t in range(tiles2):
        u2[t] = u2[t] + dot(wider, up_lanes(t, ny2))
    two_level.smooth()

    window = a1.shape[2]
    pick = up_rows(window, all2, w * rows2 - SIDE // 2)
    grown = [dot(pick, u2[t]) for t in range(tiles2)]
    mid_sent(2)
    mid_recv(2)
    ups1 = [up_lanes(i, ny1) for i in range(4)]
    for t in range(a1.shape[1]):
        u1[PAD + t] = u1r[t] + dot(grown[t // 4], ups1[t % 4])
    one_level.smooth()

    pick0 = up_rows(bx + 2 * SIDE, window, SIDE // 2)
    ups0 = [up_lanes(i, LANES) for i in (0, 2)]
    fine_sent(1)
    fine_recv(1)
    grown0 = {}
    for zi in range(2 * DEEP + bz):
        rel = zi - DEEP
        key = rel // 4
        if key not in grown0:
            grown0[key] = dot(pick0, u1[PAD + n * tiles_own + key])
        side = (rel % 4) // 2
        if (key, side) not in grown0:
            grown0[(key, side)] = dot(grown0[key], ups0[side])
        p0[2, zi] = u0r[zi] + grown0[(key, side)]
    zero_level.smooth()
    for z in range(bz):
        pressure[:, z, :] = p0[2, DEEP + z, SIDE:SIDE + bx, :]
        residual[:, z, :] = zero_level.defect(DEEP + z)[SIDE:SIDE + bx]

    mid_sent(0)
    mid_sent(1)
    each_top(lambda step: top(0, step).wait_send())
    each_top(lambda step: top(1, step).wait_send())


def local(wide, narrow, rhs, coefficient, guess):
    bx, bz, by = rhs.shape
    hx = bx // 2
    z0 = bz + 2 * DEEP
    x0 = bx + 2 * SIDE
    t1 = narrow * bz // 4
    x1 = hx + 2 * SIDE
    t2 = t1 // 4
    x2 = wide * bx // 4
    x3 = x2 // 2
    vmem = lambda *shape: pltpu.VMEM(shape, jnp.float32)
    dma = lambda *shape: pltpu.SemaphoreType.DMA(shape)
    out = jax.ShapeDtypeStruct(rhs.shape, jnp.float32)
    return pl.pallas_call(
        functools.partial(kernel, wide, narrow),
        out_shape=(out, out),
        in_specs=[pl.BlockSpec(memory_space=pltpu.VMEM)] * 3,
        out_specs=[pl.BlockSpec(memory_space=pltpu.VMEM)] * 2,
        scratch_shapes=[
            vmem(3, z0, x0, by), vmem(z0, x0, by), vmem(6, z0, x0, by),
            vmem(2, t1, x1, LANES), vmem(t1, x1, LANES), vmem(t1 + 2 * PAD, x1, LANES), vmem(6, t1, x1, LANES),
            vmem(2, t2, x2, LANES), vmem(2, t2 * hx // 2, LANES), vmem(2, wide, t2 * hx // 2, LANES),
            vmem(t2, x2, LANES), vmem(6, t2, x2, LANES),
            vmem(2, 1, x3, LANES), vmem(6, 1, x3, LANES),
            dma(2, 9), dma(2, 9), dma(3, 3, narrow), dma(3, 3, narrow), dma(2, wide), dma(2, wide),
        ],
        compiler_params=pltpu.CompilerParams(collective_id=0, has_side_effects=True, vmem_limit_bytes=48 * 2**20),
    )(rhs, coefficient, guess)


def solution(mesh):
    spec = P("wide", "narrow", None)
    return jax.shard_map(
        functools.partial(local, mesh.shape["wide"], mesh.shape["narrow"]),
        mesh=mesh,
        in_specs=(spec, spec, spec),
        out_specs=(spec, spec),
        check_vma=False,
    )
```

time: 974 us -> 47.8 us (0.05)
  the two profiles are of different devices: /device:TPU:9 before, /device:TPU:0 now
where the time goes in v1:
time: 47.8 us; the launch traced here: 47.6 us
  Pallas kernels  43.1 us (90%)
  local copies, waits for them, and re-layouts  3.77 us (8%)
  between operations  0.65 us (1%)
    pallas_call x1, Pallas kernels, local(): pl.pallas_call(functools.partial(kernel, wide, narrow), out_shape=(out, o...  43.1 us
    unnamed x8, local copies, waits for them, and re-layouts  3.77 us

profile of v1, /device:TPU:0, one launch (start us, length us, event | category | flops | bytes accessed | tf_op | source)
XLA Modules:
  0.0 47.6 jit_solution(14524915926303824037)
XLA Ops:
  0.6 0.0 copy-start
  0.6 0.8 %copy-done = f32[16,8,128]{2,1,0:T(8,128)S(1)} copy-done((f32[16,8,128]{2,1,0:T(8,128)S(1)}, f32[16,8,128]{2,1,0:T(8,128)}, u32[]{:S(2)}) %copy-start) | copy-done | bytes 65560
  1.5 0.0 copy-start.1
  1.5 0.8 %copy-done.1 = f32[16,8,128]{2,1,0:T(8,128)S(1)} copy-done((f32[16,8,128]{2,1,0:T(8,128)S(1)}, f32[16,8,128]{2,1,0:T(8,128)}, u32[]{:S(2)}) %copy-start.1) | copy-done | bytes 65560
  2.3 0.0 copy-start.2
  2.3 0.8 %copy-done.2 = f32[16,8,128]{2,1,0:T(8,128)S(1)} copy-done((f32[16,8,128]{2,1,0:T(8,128)S(1)}, f32[16,8,128]{2,1,0:T(8,128)}, u32[]{:S(2)}) %copy-start.2) | copy-done | bytes 65560
  3.2 43.1 %shard_map.50 = (f32[16,8,128]{2,1,0:T(8,128)S(1)}, f32[16,8,128]{2,1,0:T(8,128)S(1)}) custom-call(f32[16,8,128]{2,1,0:T(8,128)S(1)} %copy-done, f32[16,8,128]{2,1,0:T(8,128)S(1)} %copy-done.1, f32[16,8,128]{2,1,0:T(8,128)S(1)} %copy-done.2), custom_call_target="tpu_custom_call" | custom-call | tf_op jit(solution)/shard_map/pallas_call | solution.py:462
  46.3 0.6 %copy.7 = f32[16,8,128]{2,1,0:T(8,128)} copy(f32[16,8,128]{2,1,0:T(8,128)S(1)} %get-tuple-element.4) | data formatting | bytes 131072
  46.9 0.6 %copy.8 = f32[16,8,128]{2,1,0:T(8,128)} copy(f32[16,8,128]{2,1,0:T(8,128)S(1)} %get-tuple-element.5) | data formatting | bytes 131072
Async XLA Ops:
  0.6 0.8 %copy-start = (f32[16,8,128]{2,1,0:T(8,128)S(1)}, f32[16,8,128]{2,1,0:T(8,128)}, u32[]{:S(2)}) copy-start(f32[16,8,128]{2,1,0:T(8,128)} %rhs.1) | copy-start | bytes 196612
  1.5 0.8 %copy-start.1 = (f32[16,8,128]{2,1,0:T(8,128)S(1)}, f32[16,8,128]{2,1,0:T(8,128)}, u32[]{:S(2)}) copy-start(f32[16,8,128]{2,1,0:T(8,128)} %cond.1) | copy-start | bytes 196612
  2.3 0.8 %copy-start.2 = (f32[16,8,128]{2,1,0:T(8,128)S(1)}, f32[16,8,128]{2,1,0:T(8,128)}, u32[]{:S(2)}) copy-start(f32[16,8,128]{2,1,0:T(8,128)} %guess.1) | copy-start | bytes 196612

commit v2 on v1

--- a/solution.py
+++ b/solution.py
@@ -63,18 +63,21 @@
         self.rows = k.shape[1]
         self.tiles = k.shape[0]
 
+    def spin(self, v):
+        if self.ny == LANES:
+            return v, v
+        down = pltpu.roll(v, LANES - self.ny, 1)
+        return down, (down if 2 * self.ny == LANES else pltpu.roll(v, self.ny, 1))
+
     def above(self, here, after):
         if self.ny == LANES:
-            return after
-        lane = iota(here.shape, 1)
-        step = LANES - self.ny
-        return jnp.where(lane < step, pltpu.roll(here, step, 1), pltpu.roll(after, step, 1))
+            return after[0]
+        return jnp.where(iota(here[0].shape, 1) < LANES - self.ny, here[0], after[0])
 
     def below(self, here, before):
         if self.ny == LANES:
-            return before
-        lane = iota(here.shape, 1)
-        return jnp.where(lane >= self.ny, pltpu.roll(here, self.ny, 1), pltpu.roll(before, self.ny, 1))
+            return before[1]
+        return jnp.where(iota(here[0].shape, 1) >= self.ny, here[1], before[1])
 
     def operator(self):
         shape = (self.rows, LANES)
@@ -83,14 +86,15 @@
         zero = jnp.zeros(shape, jnp.float32)
         for t in range(self.first, self.last):
             k = self.k[t]
-            after = self.k[t + 1] if t + 1 < self.tiles else zero
-            before = self.k[t - 1] if t > 0 else zero
+            spun = self.spin(k)
+            after = self.spin(self.k[t + 1] if t + 1 < self.tiles else zero)
+            before = self.spin(self.k[t - 1] if t > 0 else zero)
             xp = jnp.where(row == self.rows - 1, 0.0, pltpu.roll(k, self.rows - 1, 0))
             xm = jnp.where(row == 0, 0.0, pltpu.roll(k, 1, 0))
             yp = jnp.where(y == self.ny - 1, 0.0, pltpu.roll(k, LANES - 1, 1))
             ym = jnp.where(y == 0, 0.0, pltpu.roll(k, 1, 1))
-            zp = self.above(k, after)
-            zm = self.below(k, before)
+            zp = self.above(spun, after)
+            zm = self.below(spun, before)
             diag = 3.0 * k + 0.5 * (xp + xm + zp + zm + yp + ym)
             diag = jnp.where(diag > 0.0, diag, 1.0)
             live = k > 0.0
@@ -105,43 +109,57 @@
             self.diag[t] = diag
             self.inv[t] = 1.0 / diag
 
-    def beside(self, t, here, after, before):
+    def beside(self, t, here, spun, after, before):
         wx = self.wx[t]
         wy = self.wy[t]
-        total = wx * pltpu.roll(here, self.rows - 1, 0) + pltpu.roll(wx * here, 1, 0)
-        total = total + (wy * pltpu.roll(here, LANES - 1, 1) + pltpu.roll(wy * here, 1, 1))
-        return total + (self.wzp[t] * self.above(here, after) + self.wzm[t] * self.below(here, before))
-
-    def around(self, t):
-        here = self.u[t + self.off]
-        after = self.u[t + 1 + self.off] if t + 1 < self.tiles else here
-        before = self.u[t - 1 + self.off] if t > 0 else here
-        return here, after, before
-
-    def smooth(self):
+        total = self.wzp[t] * self.above(spun, after) + self.wzm[t] * self.below(spun, before)
+        total = total + (wx * pltpu.roll(here, self.rows - 1, 0) + pltpu.roll(wx * here, 1, 0))
+        return total + (wy * pltpu.roll(here, LANES - 1, 1) + pltpu.roll(wy * here, 1, 1))
+
+    def sides(self, first, last):
+        here = self.u[first + self.off]
+        spun = self.spin(here)
+        before = self.spin(self.u[first - 1 + self.off]) if first > 0 else spun
+        for t in range(first, last):
+            if t + 1 < self.tiles:
+                later = self.u[t + 1 + self.off]
+                after = self.spin(later)
+            else:
+                later, after = here, spun
+            yield t, here, spun, after, before
+            here, before, spun = later, spun, after
+
+    def half_sweep(self, step, first, last):
         shape = (self.rows, LANES)
         shift = self.ny.bit_length() - 1
         lane = iota(shape, 1)
-        place = iota(shape, 0) + (lane >> shift) + (lane & (self.ny - 1)) + self.odd
-
-        @pl.loop(0, 4)
-        def _(step):
-            even = ((place + step) & 1) == 0
-            other = ((place + step) & 1) == 1
-            for t in range(self.first, self.last):
-                here, after, before = self.around(t)
-                fresh = (self.f[t] + self.beside(t, here, after, before)) * self.inv[t]
-                mask = other if (self.ny == LANES and t % 2 == 1) else even
-                self.u[t + self.off] = jnp.where(mask, fresh, here)
-
-    def defect(self, t):
-        here, after, before = self.around(t)
-        return self.f[t] - (self.diag[t] * here - self.beside(t, here, after, before))
+        place = iota(shape, 0) + (lane >> shift) + (lane & (self.ny - 1)) + self.odd + step
+        even = (place & 1) == 0
+        other = (place & 1) == 1
+        for t, here, spun, after, before in self.sides(first, last):
+            fresh = (self.f[t] + self.beside(t, here, spun, after, before)) * self.inv[t]
+            mask = other if (self.ny == LANES and t % 2 == 1) else even
+            self.u[t + self.off] = jnp.where(mask, fresh, here)
+
+    def smooth(self):
+        if self.ny == LANES:
+            for step in range(4):
+                self.half_sweep(step, self.first + step, self.last - step)
+        else:
+            @pl.loop(0, 4)
+            def _(step):
+                self.half_sweep(step, self.first, self.last)
+
+    def defects(self, first, last):
+        return [
+            self.f[t] - (self.diag[t] * here - self.beside(t, here, spun, after, before))
+            for t, here, spun, after, before in self.sides(first, last)
+        ]
 
 
 def kernel(wide, narrow, rhs, cond, guess, pressure, residual, *scratch):
-    (p0, u0r, op0, a1, u1r, u1, op1, a2, own2, g2, u2, op2, a3, op3,
-     send0, recv0, send1, recv1, send2, recv2) = scratch
+    (ins, p0, u0r, op0, a1, u1r, u1, op1, a2, own2, g2, u2, op2, a3, op3,
+     in_sem, send0, recv0, send1, recv1, send2, recv2) = scratch
     w = lax.axis_index("wide")
     n = lax.axis_index("narrow")
     bx, bz, _ = rhs.shape
@@ -151,6 +169,10 @@
     tiles_own = hz // 2
     f32 = jnp.float32
 
+    loads = [pltpu.make_async_copy(ref, ins.at[i], in_sem.at[i]) for i, ref in enumerate((cond, rhs, guess))]
+    for load in loads:
+        load.start()
+
     for ref in (p0, u0r, a1, u1r):
         ref[...] = jnp.zeros(ref.shape, f32)
     u1[...] = jnp.zeros(u1.shape, f32)
@@ -183,10 +205,10 @@
         def _():
             greet((other, n))
 
-    for z in range(bz):
-        p0[0, DEEP + z, SIDE:SIDE + bx, :] = cond[:, z, :]
-        p0[1, DEEP + z, SIDE:SIDE + bx, :] = rhs[:, z, :]
-        p0[2, DEEP + z, SIDE:SIDE + bx, :] = guess[:, z, :]
+    for i in range(3):
+        loads[i].wait()
+        for z in range(bz):
+            p0[i, DEEP + z, SIDE:SIDE + bx, :] = ins[i, :, z, :]
 
     half = down_rows(bx)
     lanes0 = [down_lanes(i, LANES) for i in (0, 2)]
@@ -218,8 +240,8 @@
     def fine(which, dw, dn):
         src_z, dst_z, len_z = zs[dn]
         src_x, dst_x, len_x = xs[dw]
-        ref = p0 if which == 0 else u0r
-        lead = (slice(None),) if which == 0 else ()
+        ref = (p0.at[0], p0.at[pl.ds(1, 2)], u0r)[which]
+        lead = (slice(None),) if which == 1 else ()
         src = ref.at[lead + (pl.ds(src_z, len_z), pl.ds(src_x, len_x))]
         dst = ref.at[lead + (pl.ds(dst_z, len_z), pl.ds(dst_x, len_x))]
         mine = (dw + 1) * 3 + dn + 1
@@ -231,8 +253,8 @@
     def fine_in(which, dw, dn):
         _, dst_z, len_z = zs[-dn]
         _, dst_x, len_x = xs[-dw]
-        ref = p0 if which == 0 else u0r
-        lead = (slice(None),) if which == 0 else ()
+        ref = (p0.at[0], p0.at[pl.ds(1, 2)], u0r)[which]
+        lead = (slice(None),) if which == 1 else ()
         dst = ref.at[lead + (pl.ds(dst_z, len_z), pl.ds(dst_x, len_x))]
         mine = (dw + 1) * 3 + dn + 1
         return pltpu.make_async_remote_copy(
@@ -306,19 +328,22 @@
             fun(step)
 
     fine_start(0)
-    mid_start(0)
+    fine_start(1)
     fine_recv(0)
 
     names = range(6)
     ny = LANES
     zero_level = Level(p0.at[0], p0.at[1], p0.at[2], *[op0.at[i] for i in names], LANES, 1, 2 * DEEP + bz - 1, odd=1)
     zero_level.operator()
+    fine_recv(1)
+    mid_start(0)
     fine_sent(0)
+    fine_sent(1)
     zero_level.smooth()
-    to_level_1(1, [zero_level.defect(DEEP + z)[SIDE:SIDE + bx] for z in range(bz)], 0.5)
+    to_level_1(1, [v[SIDE:SIDE + bx] for v in zero_level.defects(DEEP, DEEP + bz)], 0.5)
     mid_start(1)
     u0r[own_z, own_x, :] = p0[2, own_z, own_x, :]
-    fine_start(1)
+    fine_start(2)
 
     ny1, ny2, ny3 = LANES // 2, LANES // 4, LANES // 8
     mid_recv(0)
@@ -346,7 +371,7 @@
     one_level.operator()
     mid_recv(1)
     one_level.smooth()
-    to_level_2(1, [one_level.defect(t)[SIDE:SIDE + hx] for t in range(a1.shape[1])], 0.5)
+    to_level_2(1, [v[SIDE:SIDE + hx] for v in one_level.defects(0, a1.shape[1])], 0.5)
     each_top(lambda step: top(1, step).start())
     u1r[pl.ds(n * tiles_own, tiles_own), SIDE:SIDE + hx, :] = u1[pl.ds(PAD + n * tiles_own, tiles_own), SIDE:SIDE + hx, :]
     mid_start(2)
@@ -377,34 +402,36 @@
     unpack(1)
     u2[...] = jnp.zeros(u2.shape, f32)
     two_level.smooth()
-    source = to_level_3([two_level.defect(t) for t in range(tiles2)], 0.5)
+    source = to_level_3(two_level.defects(0, tiles2), 0.5)
 
     def image(v):
-        return last.diag[0] * v - last.beside(0, v, v, v)
+        spun = last.spin(v)
+        return last.diag[0] * v - last.beside(0, v, spun, spun, spun)
 
     def total(v):
         return jnp.sum(jnp.sum(v, axis=0, keepdims=True), axis=1, keepdims=True)
 
-    first_image = image(source)
-    rr = total(source * source)
-    alpha = rr / total(source * first_image)
-
     def advance(step, carry):
-        answer, remain, search, moved, norm, alpha = carry
+        answer, remain, wave, search, moved, twice, norm, rate = carry
+        norm_next = total(remain * remain)
+        cross = total(wave * remain)
+        ahead = image(wave)
+        beta = jnp.where(step == 0, 0.0, norm_next / norm)
+        below = cross - beta * (norm_next * rate)
+        alpha = norm_next / below
+        rate = below / norm_next
+        twice = ahead + beta * twice
+        moved = wave + beta * moved
+        search = remain + beta * search
         answer = answer + alpha * search
         remain = remain - alpha * moved
-        fresh = image(remain)
-        norm_next = total(remain * remain)
-        cross = total(remain * fresh)
-        beta = norm_next / norm
-        alpha_next = norm_next / (cross - beta * norm_next / alpha)
-        search = remain + beta * search
-        moved = fresh + beta * moved
-        return answer, remain, search, moved, norm_next, alpha_next
-
-    carry = (jnp.zeros_like(source), source, source, first_image, rr, alpha)
-    carry = lax.fori_loop(0, ITERS - 1, advance, carry)
-    solved = carry[0] + carry[5] * carry[2]
+        wave = wave - alpha * twice
+        return answer, remain, wave, search, moved, twice, norm_next, rate
+
+    nothing = jnp.zeros_like(source)
+    unit = jnp.ones((1, 1), f32)
+    carry = (nothing, source, image(source), nothing, nothing, nothing, unit, unit)
+    solved = lax.fori_loop(0, ITERS, advance, carry)[0]
 
     wider = dot(up_rows(all2, all3, 0), solved)
     for t in range(tiles2):
@@ -423,8 +450,8 @@
 
     pick0 = up_rows(bx + 2 * SIDE, window, SIDE // 2)
     ups0 = [up_lanes(i, LANES) for i in (0, 2)]
-    fine_sent(1)
-    fine_recv(1)
+    fine_sent(2)
+    fine_recv(2)
     grown0 = {}
     for zi in range(2 * DEEP + bz):
         rel = zi - DEEP
@@ -436,9 +463,9 @@
             grown0[(key, side)] = dot(grown0[key], ups0[side])
         p0[2, zi] = u0r[zi] + grown0[(key, side)]
     zero_level.smooth()
-    for z in range(bz):
+    for z, left in enumerate(zero_level.defects(DEEP, DEEP + bz)):
         pressure[:, z, :] = p0[2, DEEP + z, SIDE:SIDE + bx, :]
-        residual[:, z, :] = zero_level.defect(DEEP + z)[SIDE:SIDE + bx]
+        residual[:, z, :] = left[SIDE:SIDE + bx]
 
     mid_sent(0)
     mid_sent(1)
@@ -462,15 +489,15 @@
     return pl.pallas_call(
         functools.partial(kernel, wide, narrow),
         out_shape=(out, out),
-        in_specs=[pl.BlockSpec(memory_space=pltpu.VMEM)] * 3,
+        in_specs=[pl.BlockSpec(memory_space=pl.ANY)] * 3,
         out_specs=[pl.BlockSpec(memory_space=pltpu.VMEM)] * 2,
         scratch_shapes=[
-            vmem(3, z0, x0, by), vmem(z0, x0, by), vmem(6, z0, x0, by),
+            vmem(3, bx, bz, by), vmem(3, z0, x0, by), vmem(z0, x0, by), vmem(6, z0, x0, by),
             vmem(2, t1, x1, LANES), vmem(t1, x1, LANES), vmem(t1 + 2 * PAD, x1, LANES), vmem(6, t1, x1, LANES),
             vmem(2, t2, x2, LANES), vmem(2, t2 * hx // 2, LANES), vmem(2, wide, t2 * hx // 2, LANES),
             vmem(t2, x2, LANES), vmem(6, t2, x2, LANES),
             vmem(2, 1, x3, LANES), vmem(6, 1, x3, LANES),
-            dma(2, 9), dma(2, 9), dma(3, 3, narrow), dma(3, 3, narrow), dma(2, wide), dma(2, wide),
+            dma(3), dma(3, 9), dma(3, 9), dma(3, 3, narrow), dma(3, 3, narrow), dma(2, wide), dma(2, wide),
         ],
         compiler_params=pltpu.CompilerParams(collective_id=0, has_side_effects=True, vmem_limit_bytes=48 * 2**20),
     )(rhs, coefficient, guess)

time: 47.8 us -> 39.9 us (0.83)
  Pallas kernels: 43.1 us -> 35.3 us
    pallas_call x1, Pallas kernels: 43.1 us -> 35.3 us  [local(): pl.pallas_call(functools.partial(kernel, wide, narrow), out_shape=(out, o...]
where the time goes in v2:
time: 39.9 us; the launch traced here: 39.7 us
  Pallas kernels  35.3 us (88%)
  local copies, waits for them, and re-layouts  3.77 us (9%)
  between operations  0.65 us (2%)
    pallas_call x1, Pallas kernels, local(): pl.pallas_call(functools.partial(kernel, wide, narrow), out_shape=(out, o...  35.3 us
    unnamed x8, local copies, waits for them, and re-layouts  3.77 us

profile of v2, /device:TPU:0, one launch (start us, length us, event | category | flops | bytes accessed | tf_op | source)
XLA Modules:
  0.0 39.7 jit_solution(14217102397117987602)
XLA Ops:
  0.6 0.0 copy-start
  0.6 0.8 %copy-done = f32[16,8,128]{2,1,0:T(8,128)S(1)} copy-done((f32[16,8,128]{2,1,0:T(8,128)S(1)}, f32[16,8,128]{2,1,0:T(8,128)}, u32[]{:S(2)}) %copy-start) | copy-done | bytes 65560
  1.5 0.0 copy-start.1
  1.5 0.8 %copy-done.1 = f32[16,8,128]{2,1,0:T(8,128)S(1)} copy-done((f32[16,8,128]{2,1,0:T(8,128)S(1)}, f32[16,8,128]{2,1,0:T(8,128)}, u32[]{:S(2)}) %copy-start.1) | copy-done | bytes 65560
  2.3 0.0 copy-start.2
  2.3 0.8 %copy-done.2 = f32[16,8,128]{2,1,0:T(8,128)S(1)} copy-done((f32[16,8,128]{2,1,0:T(8,128)S(1)}, f32[16,8,128]{2,1,0:T(8,128)}, u32[]{:S(2)}) %copy-start.2) | copy-done | bytes 65560
  3.2 35.3 %shard_map.50 = (f32[16,8,128]{2,1,0:T(8,128)S(1)}, f32[16,8,128]{2,1,0:T(8,128)S(1)}) custom-call(f32[16,8,128]{2,1,0:T(8,128)S(1)} %copy-done, f32[16,8,128]{2,1,0:T(8,128)S(1)} %copy-done.1, f32[16,8,128]{2,1,0:T(8,128)S(1)} %copy-done.2), custom_call_target="tpu_custom_call" | custom-call | tf_op jit(solution)/shard_map/pallas_call | solution.py:489
  38.4 0.6 %copy.7 = f32[16,8,128]{2,1,0:T(8,128)} copy(f32[16,8,128]{2,1,0:T(8,128)S(1)} %get-tuple-element.4) | data formatting | bytes 131072
  39.1 0.6 %copy.8 = f32[16,8,128]{2,1,0:T(8,128)} copy(f32[16,8,128]{2,1,0:T(8,128)S(1)} %get-tuple-element.5) | data formatting | bytes 131072
Async XLA Ops:
  0.6 0.8 %copy-start = (f32[16,8,128]{2,1,0:T(8,128)S(1)}, f32[16,8,128]{2,1,0:T(8,128)}, u32[]{:S(2)}) copy-start(f32[16,8,128]{2,1,0:T(8,128)} %rhs.1) | copy-start | bytes 196612
  1.5 0.8 %copy-start.1 = (f32[16,8,128]{2,1,0:T(8,128)S(1)}, f32[16,8,128]{2,1,0:T(8,128)}, u32[]{:S(2)}) copy-start(f32[16,8,128]{2,1,0:T(8,128)} %cond.1) | copy-start | bytes 196612
  2.3 0.8 %copy-start.2 = (f32[16,8,128]{2,1,0:T(8,128)S(1)}, f32[16,8,128]{2,1,0:T(8,128)}, u32[]{:S(2)}) copy-start(f32[16,8,128]{2,1,0:T(8,128)} %guess.1) | copy-start | bytes 196612

commit v3 on v2

--- a/solution.py
+++ b/solution.py
@@ -16,9 +16,32 @@
 
 
 def dot(a, b):
-    return lax.dot_general(
-        a, b, (((1,), (0,)), ((), ())), precision=lax.Precision.HIGHEST, preferred_element_type=jnp.float32
-    )
+    return lax.dot_general(a, b, (((1,), (0,)), ((), ())), preferred_element_type=jnp.float32)
+
+
+def split(a):
+    high = a.astype(jnp.bfloat16).astype(jnp.float32)
+    rest = a - high
+    mid = rest.astype(jnp.bfloat16).astype(jnp.float32)
+    return jnp.concatenate([high, mid, rest - mid], axis=0).astype(jnp.bfloat16)
+
+
+def map_lanes(a, matrix):
+    rows = a.shape[0]
+    out = dot(split(a), matrix)
+    return out[:rows] + (out[rows:2 * rows] + out[2 * rows:])
+
+
+def map_rows(matrix, a):
+    return dot(jnp.concatenate([matrix, matrix, matrix], axis=1).astype(jnp.bfloat16), split(a))
+
+
+def beside_each(parts):
+    return jnp.concatenate(parts, axis=1)
+
+
+def stacked(parts):
+    return jnp.concatenate(parts, axis=0)
 
 
 def iota(shape, dim):
@@ -158,7 +181,7 @@
 
 
 def kernel(wide, narrow, rhs, cond, guess, pressure, residual, *scratch):
-    (ins, p0, u0r, op0, a1, u1r, u1, op1, a2, own2, g2, u2, op2, a3, op3,
+    (ins, p0, u0r, op0, a1, u1r, u1, op1, a2, own2, g2, u2, op2, a3, op3, down0, up0, down1, up1, down2, up2,
      in_sem, send0, recv0, send1, recv1, send2, recv2) = scratch
     w = lax.axis_index("wide")
     n = lax.axis_index("narrow")
@@ -210,16 +233,13 @@
         for z in range(bz):
             p0[i, DEEP + z, SIDE:SIDE + bx, :] = ins[i, :, z, :]
 
-    half = down_rows(bx)
-    lanes0 = [down_lanes(i, LANES) for i in (0, 2)]
-
     def to_level_1(index, slices, factor):
+        pairs = beside_each([slices[2 * i] + slices[2 * i + 1] for i in range(hz)])
+        thin = map_rows(down_rows(bx), pairs)
+        flat = stacked([thin[:, 2 * LANES * tt:2 * LANES * (tt + 1)] for tt in range(tiles_own)])
+        done = factor * map_lanes(flat, down0[...])
         for tt in range(tiles_own):
-            four = [slices[4 * tt + i] for i in range(4)]
-            spread = dot(four[0] + four[1], lanes0[0]) + dot(four[2] + four[3], lanes0[1])
-            a1[index, n * tiles_own + tt, SIDE:SIDE + hx, :] = factor * dot(half, spread)
-
-    to_level_1(0, [p0[0, DEEP + z, SIDE:SIDE + bx, :] for z in range(bz)], 0.125)
+            a1[index, n * tiles_own + tt, SIDE:SIDE + hx, :] = done[hx * tt:hx * (tt + 1)]
 
     near = jnp.where(w > 0, 1, 0) + jnp.where(w < wide - 1, 1, 0)
     pl.semaphore_wait(barrier, (wide - 1 - near) + near * narrow + narrow - 1)
@@ -329,10 +349,19 @@
 
     fine_start(0)
     fine_start(1)
+
+    names = range(6)
+    ny1, ny2, ny3 = LANES // 2, LANES // 4, LANES // 8
+    tiles2 = a1.shape[1] // 4
+    bf16 = jnp.bfloat16
+    down0[...] = stacked([down_lanes(i, LANES) for i in (0, 2)]).astype(bf16)
+    up0[...] = beside_each([up_lanes(i, LANES) for i in (0, 2)]).astype(bf16)
+    down1[...] = stacked([down_lanes(i, ny1) for i in range(4)]).astype(bf16)
+    up1[...] = beside_each([up_lanes(i, ny1) for i in range(4)]).astype(bf16)
+    down2[...] = stacked([down_lanes(i, ny2) for i in range(tiles2)]).astype(bf16)
+    up2[...] = beside_each([up_lanes(i, ny2) for i in range(tiles2)]).astype(bf16)
+    to_level_1(0, [p0[0, DEEP + z, SIDE:SIDE + bx, :] for z in range(bz)], 0.125)
     fine_recv(0)
-
-    names = range(6)
-    ny = LANES
     zero_level = Level(p0.at[0], p0.at[1], p0.at[2], *[op0.at[i] for i in names], LANES, 1, 2 * DEEP + bz - 1, odd=1)
     zero_level.operator()
     fine_recv(1)
@@ -345,24 +374,13 @@
     u0r[own_z, own_x, :] = p0[2, own_z, own_x, :]
     fine_start(2)
 
-    ny1, ny2, ny3 = LANES // 2, LANES // 4, LANES // 8
     mid_recv(0)
     one_level = Level(a1.at[0], a1.at[1], u1, *[op1.at[i] for i in names], ny1, 0, a1.shape[1], off=PAD)
     rows2 = hx // 2
-    lanes1 = [down_lanes(i, ny1) for i in range(4)]
-    tiles2 = a1.shape[1] // 4
 
     def to_level_2(which, tiles, factor):
-        shape = (tiles2 * rows2, hx)
-        pack = None
-        for big in range(tiles2):
-            spread = dot(tiles[4 * big], lanes1[0])
-            for i in range(1, 4):
-                spread = spread + dot(tiles[4 * big + i], lanes1[i])
-            place = one(iota(shape, 0) == (iota(shape, 1) >> 1) + big * rows2)
-            part = dot(place, spread)
-            pack = part if pack is None else pack + part
-        pack = factor * pack
+        flat = stacked([beside_each(tiles[4 * big:4 * big + 4]) for big in range(tiles2)])
+        pack = factor * map_rows(down_rows(tiles2 * hx), map_lanes(flat, down1[...]))
         own2[which] = pack
         g2[which, w] = pack
 
@@ -386,14 +404,9 @@
     two_level = Level(a2.at[0], a2.at[1], u2, *[op2.at[i] for i in names], ny2, 0, tiles2)
     two_level.operator()
     all2, all3 = a2.shape[2], a3.shape[2]
-    half2 = down_rows(all2)
-    lanes2 = [down_lanes(i, ny2) for i in range(tiles2)]
 
     def to_level_3(tiles, factor):
-        spread = dot(tiles[0], lanes2[0])
-        for i in range(1, tiles2):
-            spread = spread + dot(tiles[i], lanes2[i])
-        return factor * dot(half2, spread)
+        return factor * map_rows(down_rows(all2), map_lanes(beside_each(tiles), down2[...]))
 
     a3[0, 0] = to_level_3([a2[0, t] for t in range(tiles2)], 0.125)
     last = Level(a3.at[0], a3.at[1], a3.at[1], *[op3.at[i] for i in names], ny3, 0, 1)
@@ -433,35 +446,33 @@
     carry = (nothing, source, image(source), nothing, nothing, nothing, unit, unit)
     solved = lax.fori_loop(0, ITERS, advance, carry)[0]
 
-    wider = dot(up_rows(all2, all3, 0), solved)
+    wider = map_lanes(map_rows(up_rows(all2, all3, 0), solved), up2[...])
     for t in range(tiles2):
-        u2[t] = u2[t] + dot(wider, up_lanes(t, ny2))
+        u2[t] = u2[t] + wider[:, LANES * t:LANES * (t + 1)]
     two_level.smooth()
 
     window = a1.shape[2]
     pick = up_rows(window, all2, w * rows2 - SIDE // 2)
-    grown = [dot(pick, u2[t]) for t in range(tiles2)]
+    thin = map_rows(pick, beside_each([u2[t] for t in range(tiles2)]))
+    grown = map_lanes(stacked([thin[:, LANES * t:LANES * (t + 1)] for t in range(tiles2)]), up1[...])
     mid_sent(2)
     mid_recv(2)
-    ups1 = [up_lanes(i, ny1) for i in range(4)]
     for t in range(a1.shape[1]):
-        u1[PAD + t] = u1r[t] + dot(grown[t // 4], ups1[t % 4])
+        big, i = t // 4, t % 4
+        u1[PAD + t] = u1r[t] + grown[window * big:window * (big + 1), LANES * i:LANES * (i + 1)]
     one_level.smooth()
 
     pick0 = up_rows(bx + 2 * SIDE, window, SIDE // 2)
-    ups0 = [up_lanes(i, LANES) for i in (0, 2)]
+    low, high = -DEEP // 4, (bz + DEEP - 1) // 4
+    thin = map_rows(pick0, beside_each([u1[PAD + n * tiles_own + key] for key in range(low, high + 1)]))
+    span = thin.shape[0]
+    grown = map_lanes(stacked([thin[:, LANES * t:LANES * (t + 1)] for t in range(high + 1 - low)]), up0[...])
     fine_sent(2)
     fine_recv(2)
-    grown0 = {}
     for zi in range(2 * DEEP + bz):
-        rel = zi - DEEP
-        key = rel // 4
-        if key not in grown0:
-            grown0[key] = dot(pick0, u1[PAD + n * tiles_own + key])
-        side = (rel % 4) // 2
-        if (key, side) not in grown0:
-            grown0[(key, side)] = dot(grown0[key], ups0[side])
-        p0[2, zi] = u0r[zi] + grown0[(key, side)]
+        t = (zi - DEEP) // 4 - low
+        side = ((zi - DEEP) % 4) // 2
+        p0[2, zi] = u0r[zi] + grown[span * t:span * (t + 1), LANES * side:LANES * (side + 1)]
     zero_level.smooth()
     for z, left in enumerate(zero_level.defects(DEEP, DEEP + bz)):
         pressure[:, z, :] = p0[2, DEEP + z, SIDE:SIDE + bx, :]
@@ -484,12 +495,13 @@
     x2 = wide * bx // 4
     x3 = x2 // 2
     vmem = lambda *shape: pltpu.VMEM(shape, jnp.float32)
+    half = lambda *shape: pltpu.VMEM(shape, jnp.bfloat16)
     dma = lambda *shape: pltpu.SemaphoreType.DMA(shape)
     out = jax.ShapeDtypeStruct(rhs.shape, jnp.float32)
     return pl.pallas_call(
         functools.partial(kernel, wide, narrow),
         out_shape=(out, out),
-        in_specs=[pl.BlockSpec(memory_space=pl.ANY)] * 3,
+        in_specs=[pl.BlockSpec(memory_space=pltpu.HBM)] * 3,
         out_specs=[pl.BlockSpec(memory_space=pltpu.VMEM)] * 2,
         scratch_shapes=[
             vmem(3, bx, bz, by), vmem(3, z0, x0, by), vmem(z0, x0, by), vmem(6, z0, x0, by),
@@ -497,6 +509,8 @@
             vmem(2, t2, x2, LANES), vmem(2, t2 * hx // 2, LANES), vmem(2, wide, t2 * hx // 2, LANES),
             vmem(t2, x2, LANES), vmem(6, t2, x2, LANES),
             vmem(2, 1, x3, LANES), vmem(6, 1, x3, LANES),
+            half(2 * LANES, LANES), half(LANES, 2 * LANES), half(4 * LANES, LANES), half(LANES, 4 * LANES),
+            half(t2 * LANES, LANES), half(LANES, t2 * LANES),
             dma(3), dma(3, 9), dma(3, 9), dma(3, 3, narrow), dma(3, 3, narrow), dma(2, wide), dma(2, wide),
         ],
         compiler_params=pltpu.CompilerParams(collective_id=0, has_side_effects=True, vmem_limit_bytes=48 * 2**20),

time: 39.9 us -> 38.6 us (0.967)
  Pallas kernels: 35.3 us -> 33.9 us
    pallas_call x1, Pallas kernels: 35.3 us -> 33.9 us  [local(): pl.pallas_call(functools.partial(kernel, wide, narrow), out_shape=(out, o...]
where the time goes in v3:
time: 38.6 us; the launch traced here: 38.3 us
  Pallas kernels  33.9 us (88%)
  local copies, waits for them, and re-layouts  3.77 us (10%)
  between operations  0.65 us (2%)
    pallas_call x1, Pallas kernels, local(): pl.pallas_call(functools.partial(kernel, wide, narrow), out_shape=(out, o...  33.9 us
    unnamed x8, local copies, waits for them, and re-layouts  3.77 us

profile of v3, /device:TPU:0, one launch (start us, length us, event | category | flops | bytes accessed | tf_op | source)
XLA Modules:
  0.0 38.3 jit_solution(5746047486957124381)
XLA Ops:
  0.6 0.0 copy-start
  0.6 0.8 %copy-done = f32[16,8,128]{2,1,0:T(8,128)S(1)} copy-done((f32[16,8,128]{2,1,0:T(8,128)S(1)}, f32[16,8,128]{2,1,0:T(8,128)}, u32[]{:S(2)}) %copy-start) | copy-done | bytes 65560
  1.5 0.0 copy-start.1
  1.5 0.8 %copy-done.1 = f32[16,8,128]{2,1,0:T(8,128)S(1)} copy-done((f32[16,8,128]{2,1,0:T(8,128)S(1)}, f32[16,8,128]{2,1,0:T(8,128)}, u32[]{:S(2)}) %copy-start.1) | copy-done | bytes 65560
  2.3 0.0 copy-start.2
  2.3 0.8 %copy-done.2 = f32[16,8,128]{2,1,0:T(8,128)S(1)} copy-done((f32[16,8,128]{2,1,0:T(8,128)S(1)}, f32[16,8,128]{2,1,0:T(8,128)}, u32[]{:S(2)}) %copy-start.2) | copy-done | bytes 65560
  3.2 33.9 %shard_map.50 = (f32[16,8,128]{2,1,0:T(8,128)S(1)}, f32[16,8,128]{2,1,0:T(8,128)S(1)}) custom-call(f32[16,8,128]{2,1,0:T(8,128)S(1)} %copy-done, f32[16,8,128]{2,1,0:T(8,128)S(1)} %copy-done.1, f32[16,8,128]{2,1,0:T(8,128)S(1)} %copy-done.2), custom_call_target="tpu_custom_call" | custom-call | tf_op jit(solution)/shard_map/pallas_call | solution.py:501
  37.1 0.6 %copy.7 = f32[16,8,128]{2,1,0:T(8,128)} copy(f32[16,8,128]{2,1,0:T(8,128)S(1)} %get-tuple-element.4) | data formatting | bytes 131072
  37.7 0.6 %copy.8 = f32[16,8,128]{2,1,0:T(8,128)} copy(f32[16,8,128]{2,1,0:T(8,128)S(1)} %get-tuple-element.5) | data formatting | bytes 131072
Async XLA Ops:
  0.6 0.8 %copy-start = (f32[16,8,128]{2,1,0:T(8,128)S(1)}, f32[16,8,128]{2,1,0:T(8,128)}, u32[]{:S(2)}) copy-start(f32[16,8,128]{2,1,0:T(8,128)} %rhs.1) | copy-start | bytes 196612
  1.5 0.8 %copy-start.1 = (f32[16,8,128]{2,1,0:T(8,128)S(1)}, f32[16,8,128]{2,1,0:T(8,128)}, u32[]{:S(2)}) copy-start(f32[16,8,128]{2,1,0:T(8,128)} %cond.1) | copy-start | bytes 196612
  2.3 0.8 %copy-start.2 = (f32[16,8,128]{2,1,0:T(8,128)S(1)}, f32[16,8,128]{2,1,0:T(8,128)}, u32[]{:S(2)}) copy-start(f32[16,8,128]{2,1,0:T(8,128)} %guess.1) | copy-start | bytes 196612

commit v4 on v3

--- a/solution.py
+++ b/solution.py
@@ -181,7 +181,7 @@
 
 
 def kernel(wide, narrow, rhs, cond, guess, pressure, residual, *scratch):
-    (ins, p0, u0r, op0, a1, u1r, u1, op1, a2, own2, g2, u2, op2, a3, op3, down0, up0, down1, up1, down2, up2,
+    (ins, corner_out, corner_in, side_in, p0, u0r, op0, a1, u1r, u1, op1, a2, own2, g2, u2, op2, a3, op3, down0, up0, down1, up1, down2, up2,
      in_sem, send0, recv0, send1, recv1, send2, recv2) = scratch
     w = lax.axis_index("wide")
     n = lax.axis_index("narrow")
@@ -241,12 +241,9 @@
         for tt in range(tiles_own):
             a1[index, n * tiles_own + tt, SIDE:SIDE + hx, :] = done[hx * tt:hx * (tt + 1)]
 
-    near = jnp.where(w > 0, 1, 0) + jnp.where(w < wide - 1, 1, 0)
-    pl.semaphore_wait(barrier, (wide - 1 - near) + near * narrow + narrow - 1)
-
     zs = {1: (DEEP + bz - DEEP, 0, DEEP), -1: (DEEP, DEEP + bz, DEEP), 0: (DEEP, DEEP, bz)}
     xs = {1: (SIDE + bx - SIDE, 0, SIDE), -1: (SIDE, SIDE + bx, SIDE), 0: (SIDE, SIDE, bx)}
-    around = [(dw, dn) for dw in (-1, 0, 1) for dn in (-1, 0, 1) if (dw, dn) != (0, 0)]
+    around = [(0, 1), (0, -1), (1, 0), (-1, 0), (1, 1), (1, -1), (-1, 1), (-1, -1)]
 
     def has(dw, dn):
         good = None
@@ -257,13 +254,49 @@
             good = zgood if good is None else good & zgood
         return good
 
-    def fine(which, dw, dn):
+    sizes = [(0, dz, DEEP - dz) for dz in range(1, DEEP)]
+    sizes += [(2, dz, DEEP - dz) for dz in range(1, DEEP)]
+    sizes += [(1, dz, DEEP - 1 - dz) for dz in range(1, DEEP - 1)]
+    slots = []
+    for which, dz, count in sizes:
+        slots.append((which, dz, count, sum(slot[2] for slot in slots)))
+    corners = [(-1, -1), (-1, 1), (1, -1), (1, 1)]
+
+    for c, (dw, dn) in enumerate(corners):
+        for i, dz, count, at in slots:
+            z = bz - dz if dn == 1 else dz - 1
+            x = bx - count if dw == 1 else 0
+            corner_out[c, at:at + count, :] = ins[i, x:x + count, z, :]
+
+    def corner_unpack(dw, dn):
+        c = corners.index((-dw, -dn))
+        for i, dz, count, at in slots:
+            z = DEEP - dz if dn == -1 else DEEP + bz + dz - 1
+            x = SIDE - count if dw == -1 else SIDE + bx
+            p0[i, z, x:x + count, :] = corner_in[c, at:at + count, :]
+
+    def side_unpack(which, dw):
+        at = SIDE - DEEP if dw == -1 else SIDE + bx
+        for i in ((0,), (1, 2))[which]:
+            for z in range(bz):
+                p0[i, DEEP + z, at:at + DEEP, :] = side_in[(dw + 1) // 2, i, :, z, :]
+
+    def fine_refs(which, dw, dn):
+        if which < 2 and dw and dn:
+            c = corners.index((dw, dn))
+            return corner_out.at[c], corner_in.at[c]
+        arrays = (pl.ds(0, 1), pl.ds(1, 2), None)[which]
+        if which < 2 and dw:
+            return ins.at[arrays, pl.ds(bx - DEEP if dw == 1 else 0, DEEP)], side_in.at[(1 - dw) // 2, arrays]
         src_z, dst_z, len_z = zs[dn]
         src_x, dst_x, len_x = xs[dw]
-        ref = (p0.at[0], p0.at[pl.ds(1, 2)], u0r)[which]
-        lead = (slice(None),) if which == 1 else ()
-        src = ref.at[lead + (pl.ds(src_z, len_z), pl.ds(src_x, len_x))]
-        dst = ref.at[lead + (pl.ds(dst_z, len_z), pl.ds(dst_x, len_x))]
+        ref = u0r if which == 2 else p0
+        lead = () if which == 2 else (arrays,)
+        return (ref.at[lead + (pl.ds(src_z, len_z), pl.ds(src_x, len_x))],
+                ref.at[lead + (pl.ds(dst_z, len_z), pl.ds(dst_x, len_x))])
+
+    def fine(which, dw, dn):
+        src, dst = fine_refs(which, dw, dn)
         mine = (dw + 1) * 3 + dn + 1
         theirs = (1 - dw) * 3 + 1 - dn
         return pltpu.make_async_remote_copy(
@@ -271,27 +304,31 @@
             device_id=(w + dw, n + dn), device_id_type=MESH)
 
     def fine_in(which, dw, dn):
-        _, dst_z, len_z = zs[-dn]
-        _, dst_x, len_x = xs[-dw]
-        ref = (p0.at[0], p0.at[pl.ds(1, 2)], u0r)[which]
-        lead = (slice(None),) if which == 1 else ()
-        dst = ref.at[lead + (pl.ds(dst_z, len_z), pl.ds(dst_x, len_x))]
+        _, dst = fine_refs(which, -dw, -dn)
         mine = (dw + 1) * 3 + dn + 1
         return pltpu.make_async_remote_copy(
             src_ref=dst, dst_ref=dst, send_sem=send0.at[which, mine], recv_sem=recv0.at[which, mine],
             device_id=(w + dw, n + dn), device_id_type=MESH)
 
+    def fine_each(which, fun):
+        for dw, dn in around:
+            if which != 1 or not (dw and dn):
+                pl.when(has(dw, dn))(lambda dw=dw, dn=dn: fun(dw, dn))
+
     def fine_start(which):
-        for dw, dn in around:
-            pl.when(has(dw, dn))(lambda dw=dw, dn=dn: fine(which, dw, dn).start())
+        fine_each(which, lambda dw, dn: fine(which, dw, dn).start())
 
     def fine_recv(which):
-        for dw, dn in around:
-            pl.when(has(dw, dn))(lambda dw=dw, dn=dn: fine_in(which, dw, dn).wait_recv())
+        def take(dw, dn):
+            fine_in(which, dw, dn).wait_recv()
+            if which < 2 and dw and dn:
+                corner_unpack(dw, dn)
+            elif which < 2 and dw:
+                side_unpack(which, dw)
+        fine_each(which, take)
 
     def fine_sent(which):
-        for dw, dn in around:
-            pl.when(has(dw, dn))(lambda dw=dw, dn=dn: fine(which, dw, dn).wait_send())
+        fine_each(which, lambda dw, dn: fine(which, dw, dn).wait_send())
 
     mid = [(dw, j) for dw in (0, -1, 1) for j in range(narrow) if (dw, j) != (0, 0)]
 
@@ -303,49 +340,55 @@
         tile = pl.ds(n * tiles_own, tiles_own)
         return pltpu.make_async_remote_copy(
             src_ref=ref.at[tile, pl.ds(SIDE, hx)], dst_ref=ref.at[tile, pl.ds(SIDE - dw * hx, hx)],
-            send_sem=send1.at[which, dw + 1, j], recv_sem=recv1.at[which, 1 - dw, j],
+            send_sem=send1.at[which, dw + 1], recv_sem=recv1.at[which, 1 - dw],
             device_id=(w + dw, lax.rem(n + j, narrow)), device_id_type=MESH)
 
-    def middle_in(which, dw, j):
-        ref = mid_ref(which)
-        src = lax.rem(n + narrow - j, narrow)
-        dst = ref.at[pl.ds(src * tiles_own, tiles_own), pl.ds(SIDE + dw * hx, hx)]
+    def middle_all(which, dw):
+        count = narrow if dw else narrow - 1
+        every = mid_ref(which).at[pl.ds(0, count * tiles_own), pl.ds(SIDE + dw * hx, hx)]
         return pltpu.make_async_remote_copy(
-            src_ref=dst, dst_ref=dst, send_sem=send1.at[which, dw + 1, j], recv_sem=recv1.at[which, dw + 1, j],
-            device_id=(w + dw, src), device_id_type=MESH)
-
-    def each_mid(fun):
+            src_ref=every, dst_ref=every, send_sem=send1.at[which, dw + 1], recv_sem=recv1.at[which, dw + 1],
+            device_id=(w + dw, lax.rem(n + 1, narrow)), device_id_type=MESH)
+
+    def mid_start(which):
         for dw, j in mid:
             if dw == 0:
-                fun(dw, j)
-            else:
-                pl.when(valid(dw))(lambda dw=dw, j=j: fun(dw, j))
-
-    def mid_start(which):
-        each_mid(lambda dw, j: middle(which, dw, j).start())
+                middle(which, dw, j).start()
+        for dw in (-1, 1):
+            @pl.when(valid(dw))
+            def _(dw=dw):
+                for j in range(narrow):
+                    middle(which, dw, j).start()
 
     def mid_recv(which):
-        each_mid(lambda dw, j: middle_in(which, dw, j).wait_recv())
+        middle_all(which, 0).wait_recv()
+        for dw in (-1, 1):
+            pl.when(valid(dw))(lambda dw=dw: middle_all(which, dw).wait_recv())
 
     def mid_sent(which):
-        each_mid(lambda dw, j: middle(which, dw, j).wait_send())
+        middle_all(which, 0).wait_send()
+        for dw in (-1, 1):
+            pl.when(valid(dw))(lambda dw=dw: middle_all(which, dw).wait_send())
 
     def top(which, step):
         other = lax.rem(w + step, wide)
         return pltpu.make_async_remote_copy(
-            src_ref=own2.at[which], dst_ref=g2.at[which, w], send_sem=send2.at[which, step],
-            recv_sem=recv2.at[which, step], device_id=(other, n), device_id_type=MESH)
-
-    def top_in(which, step):
-        src = lax.rem(w + wide - step, wide)
+            src_ref=own2.at[which], dst_ref=g2.at[which, w], send_sem=send2.at[which],
+            recv_sem=recv2.at[which], device_id=(other, n), device_id_type=MESH)
+
+    def top_all(which):
+        every = g2.at[which, pl.ds(0, wide - 1)]
         return pltpu.make_async_remote_copy(
-            src_ref=own2.at[which], dst_ref=g2.at[which, src], send_sem=send2.at[which, step],
-            recv_sem=recv2.at[which, step], device_id=(src, n), device_id_type=MESH)
-
-    def each_top(fun):
+            src_ref=every, dst_ref=every, send_sem=send2.at[which], recv_sem=recv2.at[which],
+            device_id=(lax.rem(w + 1, wide), n), device_id_type=MESH)
+
+    def top_start(which):
         @pl.loop(1, wide)
         def _(step):
-            fun(step)
+            top(which, step).start()
+
+    near = jnp.where(w > 0, 1, 0) + jnp.where(w < wide - 1, 1, 0)
+    pl.semaphore_wait(barrier, (wide - 1 - near) + near * narrow + narrow - 1)
 
     fine_start(0)
     fine_start(1)
@@ -372,7 +415,6 @@
     to_level_1(1, [v[SIDE:SIDE + bx] for v in zero_level.defects(DEEP, DEEP + bz)], 0.5)
     mid_start(1)
     u0r[own_z, own_x, :] = p0[2, own_z, own_x, :]
-    fine_start(2)
 
     mid_recv(0)
     one_level = Level(a1.at[0], a1.at[1], u1, *[op1.at[i] for i in names], ny1, 0, a1.shape[1], off=PAD)
@@ -385,21 +427,20 @@
         g2[which, w] = pack
 
     to_level_2(0, [a1[0, t, SIDE:SIDE + hx, :] for t in range(a1.shape[1])], 0.125)
-    each_top(lambda step: top(0, step).start())
+    top_start(0)
     one_level.operator()
     mid_recv(1)
     one_level.smooth()
     to_level_2(1, [v[SIDE:SIDE + hx] for v in one_level.defects(0, a1.shape[1])], 0.5)
-    each_top(lambda step: top(1, step).start())
+    top_start(1)
     u1r[pl.ds(n * tiles_own, tiles_own), SIDE:SIDE + hx, :] = u1[pl.ds(PAD + n * tiles_own, tiles_own), SIDE:SIDE + hx, :]
-    mid_start(2)
 
     def unpack(which):
         for other in range(wide):
             for t in range(tiles2):
                 a2[which, t, other * rows2:(other + 1) * rows2, :] = g2[which, other, t * rows2:(t + 1) * rows2, :]
 
-    each_top(lambda step: top_in(0, step).wait_recv())
+    top_all(0).wait_recv()
     unpack(0)
     two_level = Level(a2.at[0], a2.at[1], u2, *[op2.at[i] for i in names], ny2, 0, tiles2)
     two_level.operator()
@@ -411,9 +452,14 @@
     a3[0, 0] = to_level_3([a2[0, t] for t in range(tiles2)], 0.125)
     last = Level(a3.at[0], a3.at[1], a3.at[1], *[op3.at[i] for i in names], ny3, 0, 1)
     last.operator()
-    each_top(lambda step: top_in(1, step).wait_recv())
+    mid_sent(0)
+    mid_sent(1)
+    top_all(0).wait_send()
+    u2[...] = jnp.zeros(u2.shape, f32)
+    top_all(1).wait_recv()
+    mid_start(2)
+    fine_start(2)
     unpack(1)
-    u2[...] = jnp.zeros(u2.shape, f32)
     two_level.smooth()
     source = to_level_3(two_level.defects(0, tiles2), 0.5)
 
@@ -422,28 +468,33 @@
         return last.diag[0] * v - last.beside(0, v, spun, spun, spun)
 
     def total(v):
-        return jnp.sum(jnp.sum(v, axis=0, keepdims=True), axis=1, keepdims=True)
+        return jnp.broadcast_to(jnp.sum(jnp.sum(v, axis=0, keepdims=True), axis=1, keepdims=True), (8, LANES))
+
+    def tall(v):
+        return jnp.concatenate([v] * (all3 // 8), axis=0)
 
     def advance(step, carry):
-        answer, remain, wave, search, moved, twice, norm, rate = carry
-        norm_next = total(remain * remain)
+        answer, remain, wave, search, moved, twice, norm_inverse, rate = carry
+        norm = total(remain * remain)
         cross = total(wave * remain)
         ahead = image(wave)
-        beta = jnp.where(step == 0, 0.0, norm_next / norm)
-        below = cross - beta * (norm_next * rate)
-        alpha = norm_next / below
-        rate = below / norm_next
+        beta = norm * norm_inverse
+        below = cross - beta * (norm * rate)
+        alpha = tall(norm / below)
+        beta = tall(beta)
+        norm_inverse = 1.0 / norm
+        rate = below * norm_inverse
         twice = ahead + beta * twice
         moved = wave + beta * moved
         search = remain + beta * search
         answer = answer + alpha * search
         remain = remain - alpha * moved
         wave = wave - alpha * twice
-        return answer, remain, wave, search, moved, twice, norm_next, rate
+        return answer, remain, wave, search, moved, twice, norm_inverse, rate
 
     nothing = jnp.zeros_like(source)
-    unit = jnp.ones((1, 1), f32)
-    carry = (nothing, source, image(source), nothing, nothing, nothing, unit, unit)
+    short = jnp.zeros((8, LANES), f32)
+    carry = (nothing, source, image(source), nothing, nothing, nothing, short, short)
     solved = lax.fori_loop(0, ITERS, advance, carry)[0]
 
     wider = map_lanes(map_rows(up_rows(all2, all3, 0), solved), up2[...])
@@ -455,6 +506,7 @@
     pick = up_rows(window, all2, w * rows2 - SIDE // 2)
     thin = map_rows(pick, beside_each([u2[t] for t in range(tiles2)]))
     grown = map_lanes(stacked([thin[:, LANES * t:LANES * (t + 1)] for t in range(tiles2)]), up1[...])
+    top_all(1).wait_send()
     mid_sent(2)
     mid_recv(2)
     for t in range(a1.shape[1]):
@@ -477,11 +529,6 @@
     for z, left in enumerate(zero_level.defects(DEEP, DEEP + bz)):
         pressure[:, z, :] = p0[2, DEEP + z, SIDE:SIDE + bx, :]
         residual[:, z, :] = left[SIDE:SIDE + bx]
-
-    mid_sent(0)
-    mid_sent(1)
-    each_top(lambda step: top(0, step).wait_send())
-    each_top(lambda step: top(1, step).wait_send())
 
 
 def local(wide, narrow, rhs, coefficient, guess):
@@ -504,14 +551,15 @@
         in_specs=[pl.BlockSpec(memory_space=pltpu.HBM)] * 3,
         out_specs=[pl.BlockSpec(memory_space=pltpu.VMEM)] * 2,
         scratch_shapes=[
-            vmem(3, bx, bz, by), vmem(3, z0, x0, by), vmem(z0, x0, by), vmem(6, z0, x0, by),
+            vmem(3, bx, bz, by), vmem(4, 32, LANES), vmem(4, 32, LANES), vmem(2, 3, DEEP, bz, by),
+            vmem(3, z0, x0, by), vmem(z0, x0, by), vmem(6, z0, x0, by),
             vmem(2, t1, x1, LANES), vmem(t1, x1, LANES), vmem(t1 + 2 * PAD, x1, LANES), vmem(6, t1, x1, LANES),
             vmem(2, t2, x2, LANES), vmem(2, t2 * hx // 2, LANES), vmem(2, wide, t2 * hx // 2, LANES),
             vmem(t2, x2, LANES), vmem(6, t2, x2, LANES),
             vmem(2, 1, x3, LANES), vmem(6, 1, x3, LANES),
             half(2 * LANES, LANES), half(LANES, 2 * LANES), half(4 * LANES, LANES), half(LANES, 4 * LANES),
             half(t2 * LANES, LANES), half(LANES, t2 * LANES),
-            dma(3), dma(3, 9), dma(3, 9), dma(3, 3, narrow), dma(3, 3, narrow), dma(2, wide), dma(2, wide),
+            dma(3), dma(3, 9), dma(3, 9), dma(3, 3), dma(3, 3), dma(2), dma(2),
         ],
         compiler_params=pltpu.CompilerParams(collective_id=0, has_side_effects=True, vmem_limit_bytes=48 * 2**20),
     )(rhs, coefficient, guess)

time: 38.6 us -> 31.7 us (0.82)
  Pallas kernels: 33.9 us -> 27 us
    pallas_call x1, Pallas kernels: 33.9 us -> 27 us  [local(): pl.pallas_call(functools.partial(kernel, wide, narrow), out_shape=(out, o...]
where the time goes in v4:
time: 31.7 us; the launch traced here: 31.4 us
  Pallas kernels  27 us (85%)
  local copies, waits for them, and re-layouts  3.77 us (12%)
  between operations  0.65 us (2%)
    pallas_call x1, Pallas kernels, local(): pl.pallas_call(functools.partial(kernel, wide, narrow), out_shape=(out, o...  27 us
    unnamed x8, local copies, waits for them, and re-layouts  3.77 us

profile of v4, /device:TPU:0, one launch (start us, length us, event | category | flops | bytes accessed | tf_op | source)
XLA Modules:
  0.0 31.4 jit_solution(1916186356874751347)
XLA Ops:
  0.6 0.0 copy-start
  0.6 0.8 %copy-done = f32[16,8,128]{2,1,0:T(8,128)S(1)} copy-done((f32[16,8,128]{2,1,0:T(8,128)S(1)}, f32[16,8,128]{2,1,0:T(8,128)}, u32[]{:S(2)}) %copy-start) | copy-done | bytes 65560
  1.5 0.0 copy-start.1
  1.5 0.8 %copy-done.1 = f32[16,8,128]{2,1,0:T(8,128)S(1)} copy-done((f32[16,8,128]{2,1,0:T(8,128)S(1)}, f32[16,8,128]{2,1,0:T(8,128)}, u32[]{:S(2)}) %copy-start.1) | copy-done | bytes 65560
  2.3 0.0 copy-start.2
  2.3 0.8 %copy-done.2 = f32[16,8,128]{2,1,0:T(8,128)S(1)} copy-done((f32[16,8,128]{2,1,0:T(8,128)S(1)}, f32[16,8,128]{2,1,0:T(8,128)}, u32[]{:S(2)}) %copy-start.2) | copy-done | bytes 65560
  3.2 27.0 %shard_map.50 = (f32[16,8,128]{2,1,0:T(8,128)S(1)}, f32[16,8,128]{2,1,0:T(8,128)S(1)}) custom-call(f32[16,8,128]{2,1,0:T(8,128)S(1)} %copy-done, f32[16,8,128]{2,1,0:T(8,128)S(1)} %copy-done.1, f32[16,8,128]{2,1,0:T(8,128)S(1)} %copy-done.2), custom_call_target="tpu_custom_call" | custom-call | tf_op jit(solution)/shard_map/pallas_call | solution.py:548
  30.2 0.6 %copy.7 = f32[16,8,128]{2,1,0:T(8,128)} copy(f32[16,8,128]{2,1,0:T(8,128)S(1)} %get-tuple-element.4) | data formatting | bytes 131072
  30.8 0.6 %copy.8 = f32[16,8,128]{2,1,0:T(8,128)} copy(f32[16,8,128]{2,1,0:T(8,128)S(1)} %get-tuple-element.5) | data formatting | bytes 131072
Async XLA Ops:
  0.6 0.8 %copy-start = (f32[16,8,128]{2,1,0:T(8,128)S(1)}, f32[16,8,128]{2,1,0:T(8,128)}, u32[]{:S(2)}) copy-start(f32[16,8,128]{2,1,0:T(8,128)} %rhs.1) | copy-start | bytes 196612
  1.5 0.8 %copy-start.1 = (f32[16,8,128]{2,1,0:T(8,128)S(1)}, f32[16,8,128]{2,1,0:T(8,128)}, u32[]{:S(2)}) copy-start(f32[16,8,128]{2,1,0:T(8,128)} %cond.1) | copy-start | bytes 196612
  2.3 0.8 %copy-start.2 = (f32[16,8,128]{2,1,0:T(8,128)S(1)}, f32[16,8,128]{2,1,0:T(8,128)}, u32[]{:S(2)}) copy-start(f32[16,8,128]{2,1,0:T(8,128)} %guess.1) | copy-start | bytes 196612

commit v5 on v4

--- a/solution.py
+++ b/solution.py
@@ -152,24 +152,34 @@
             yield t, here, spun, after, before
             here, before, spun = later, spun, after
 
-    def half_sweep(self, step, first, last):
+    def half_sweep(self, step, first, last, blank=False):
         shape = (self.rows, LANES)
         shift = self.ny.bit_length() - 1
         lane = iota(shape, 1)
         place = iota(shape, 0) + (lane >> shift) + (lane & (self.ny - 1)) + self.odd + step
         even = (place & 1) == 0
         other = (place & 1) == 1
+        if blank:
+            for t in range(first, last):
+                self.u[t + self.off] = jnp.where(even, self.f[t] * self.inv[t], 0.0)
+            return
         for t, here, spun, after, before in self.sides(first, last):
             fresh = (self.f[t] + self.beside(t, here, spun, after, before)) * self.inv[t]
             mask = other if (self.ny == LANES and t % 2 == 1) else even
             self.u[t + self.off] = jnp.where(mask, fresh, here)
 
-    def smooth(self):
+    def smooth(self, blank=False):
         if self.ny == LANES:
             for step in range(4):
                 self.half_sweep(step, self.first + step, self.last - step)
+            return
+        if blank:
+            self.half_sweep(0, self.first, self.last, blank=True)
+        if self.rows <= 64:
+            for step in range(1 if blank else 0, 4):
+                self.half_sweep(step, self.first, self.last)
         else:
-            @pl.loop(0, 4)
+            @pl.loop(1 if blank else 0, 4)
             def _(step):
                 self.half_sweep(step, self.first, self.last)
 
@@ -196,10 +206,6 @@
     for load in loads:
         load.start()
 
-    for ref in (p0, u0r, a1, u1r):
-        ref[...] = jnp.zeros(ref.shape, f32)
-    u1[...] = jnp.zeros(u1.shape, f32)
-
     def valid(dw):
         return (w + dw >= 0) & (w + dw < wide)
 
@@ -228,6 +234,22 @@
         def _():
             greet((other, n))
 
+    def clear(ref):
+        ref[...] = jnp.zeros(ref.shape, f32)
+
+    lower, upper = pl.ds(0, SIDE), pl.ds(SIDE + bx, SIDE)
+    clear(p0.at[:, :, lower])
+    clear(p0.at[:, :, upper])
+    pl.when(n == 0)(lambda: clear(p0.at[:, pl.ds(0, DEEP), own_x]))
+    pl.when(n == narrow - 1)(lambda: clear(p0.at[:, pl.ds(DEEP + bz, DEEP), own_x]))
+    for at, dw in ((0, -1), (SIDE + hx, 1)):
+        @pl.when(jnp.logical_not(valid(dw)))
+        def _(at=at):
+            clear(a1.at[:, :, pl.ds(at, SIDE)])
+            clear(u1r.at[:, pl.ds(at, SIDE)])
+    clear(u1.at[pl.ds(0, PAD)])
+    clear(u1.at[pl.ds(PAD + u1r.shape[0], PAD)])
+
     for i in range(3):
         loads[i].wait()
         for z in range(bz):
@@ -243,7 +265,7 @@
 
     zs = {1: (DEEP + bz - DEEP, 0, DEEP), -1: (DEEP, DEEP + bz, DEEP), 0: (DEEP, DEEP, bz)}
     xs = {1: (SIDE + bx - SIDE, 0, SIDE), -1: (SIDE, SIDE + bx, SIDE), 0: (SIDE, SIDE, bx)}
-    around = [(0, 1), (0, -1), (1, 0), (-1, 0), (1, 1), (1, -1), (-1, 1), (-1, -1)]
+    around = [(1, 0), (-1, 0), (1, 1), (1, -1), (-1, 1), (-1, -1), (0, 1), (0, -1)]
 
     def has(dw, dn):
         good = None
@@ -330,8 +352,6 @@
     def fine_sent(which):
         fine_each(which, lambda dw, dn: fine(which, dw, dn).wait_send())
 
-    mid = [(dw, j) for dw in (0, -1, 1) for j in range(narrow) if (dw, j) != (0, 0)]
-
     def mid_ref(which):
         return u1r if which == 2 else a1.at[which]
 
@@ -351,14 +371,13 @@
             device_id=(w + dw, lax.rem(n + 1, narrow)), device_id_type=MESH)
 
     def mid_start(which):
-        for dw, j in mid:
-            if dw == 0:
-                middle(which, dw, j).start()
         for dw in (-1, 1):
             @pl.when(valid(dw))
             def _(dw=dw):
                 for j in range(narrow):
                     middle(which, dw, j).start()
+        for j in range(1, narrow):
+            middle(which, 0, j).start()
 
     def mid_recv(which):
         middle_all(which, 0).wait_recv()
@@ -392,6 +411,8 @@
 
     fine_start(0)
     fine_start(1)
+    for dw, dn in around:
+        pl.when(jnp.logical_not(has(dw, dn)))(lambda dw=dw, dn=dn: clear(fine_refs(2, -dw, -dn)[1]))
 
     names = range(6)
     ny1, ny2, ny3 = LANES // 2, LANES // 4, LANES // 8
@@ -430,7 +451,7 @@
     top_start(0)
     one_level.operator()
     mid_recv(1)
-    one_level.smooth()
+    one_level.smooth(blank=True)
     to_level_2(1, [v[SIDE:SIDE + hx] for v in one_level.defects(0, a1.shape[1])], 0.5)
     top_start(1)
     u1r[pl.ds(n * tiles_own, tiles_own), SIDE:SIDE + hx, :] = u1[pl.ds(PAD + n * tiles_own, tiles_own), SIDE:SIDE + hx, :]
@@ -455,12 +476,11 @@
     mid_sent(0)
     mid_sent(1)
     top_all(0).wait_send()
-    u2[...] = jnp.zeros(u2.shape, f32)
     top_all(1).wait_recv()
     mid_start(2)
     fine_start(2)
     unpack(1)
-    two_level.smooth()
+    two_level.smooth(blank=True)
     source = to_level_3(two_level.defects(0, tiles2), 0.5)
 
     def image(v):
@@ -526,9 +546,15 @@
         side = ((zi - DEEP) % 4) // 2
         p0[2, zi] = u0r[zi] + grown[span * t:span * (t + 1), LANES * side:LANES * (side + 1)]
     zero_level.smooth()
+    stores = [pltpu.make_async_copy(ins.at[i], ref, in_sem.at[i]) for i, ref in enumerate((pressure, residual))]
+    for z in range(bz):
+        ins[0, :, z, :] = p0[2, DEEP + z, SIDE:SIDE + bx, :]
+    stores[0].start()
     for z, left in enumerate(zero_level.defects(DEEP, DEEP + bz)):
-        pressure[:, z, :] = p0[2, DEEP + z, SIDE:SIDE + bx, :]
-        residual[:, z, :] = left[SIDE:SIDE + bx]
+        ins[1, :, z, :] = left[SIDE:SIDE + bx]
+    stores[1].start()
+    for store in stores:
+        store.wait()
 
 
 def local(wide, narrow, rhs, coefficient, guess):
@@ -549,7 +575,7 @@
         functools.partial(kernel, wide, narrow),
         out_shape=(out, out),
         in_specs=[pl.BlockSpec(memory_space=pltpu.HBM)] * 3,
-        out_specs=[pl.BlockSpec(memory_space=pltpu.VMEM)] * 2,
+        out_specs=[pl.BlockSpec(memory_space=pltpu.HBM)] * 2,
         scratch_shapes=[
             vmem(3, bx, bz, by), vmem(4, 32, LANES), vmem(4, 32, LANES), vmem(2, 3, DEEP, bz, by),
             vmem(3, z0, x0, by), vmem(z0, x0, by), vmem(6, z0, x0, by),
@@ -561,7 +587,7 @@
             half(t2 * LANES, LANES), half(LANES, t2 * LANES),
             dma(3), dma(3, 9), dma(3, 9), dma(3, 3), dma(3, 3), dma(2), dma(2),
         ],
-        compiler_params=pltpu.CompilerParams(collective_id=0, has_side_effects=True, vmem_limit_bytes=48 * 2**20),
+        compiler_params=pltpu.CompilerParams(collective_id=0, has_side_effects=True, vmem_limit_bytes=64 * 2**20 - 2**18),
     )(rhs, coefficient, guess)
 
 

time: 31.7 us -> 29.6 us (0.934)
  local copies, waits for them, and re-layouts: 3.77 us -> 2.14 us
  Pallas kernels: 27 us -> 26.6 us
    unnamed x8 -> x4, local copies, waits for them, and re-layouts: 3.77 us -> 2.14 us
    pallas_call x1, Pallas kernels: 27 us -> 26.6 us  [local(): pl.pallas_call(functools.partial(kernel, wide, narrow), out_shape=(out, o...]
where the time goes in v5:
time: 29.6 us; the launch traced here: 29.4 us
  Pallas kernels  26.6 us (90%)
  local copies, waits for them, and re-layouts  2.14 us (7%)
  between operations  0.65 us (2%)
    pallas_call x1, Pallas kernels, local(): pl.pallas_call(functools.partial(kernel, wide, narrow), out_shape=(out, o...  26.6 us
    unnamed x4, local copies, waits for them, and re-layouts  2.14 us

profile of v5, /device:TPU:0, one launch (start us, length us, event | category | flops | bytes accessed | tf_op | source)
XLA Modules:
  0.0 29.4 jit_solution(16785074808081036274)
XLA Ops:
  0.6 26.6 %shard_map.50 = (f32[16,8,128]{2,1,0:T(8,128)}, f32[16,8,128]{2,1,0:T(8,128)}) custom-call(f32[16,8,128]{2,1,0:T(8,128)} %rhs.1, f32[16,8,128]{2,1,0:T(8,128)} %cond.1, f32[16,8,128]{2,1,0:T(8,128)} %guess.1), custom_call_target="tpu_custom_call" | custom-call | tf_op jit(solution)/shard_map/pallas_call | solution.py:574
  27.2 0.0 copy-start
  27.3 1.5 %copy.7 = f32[16,8,128]{2,1,0:T(8,128)} copy(f32[16,8,128]{2,1,0:T(8,128)} %get-tuple-element.4) | data formatting | bytes 131072
  28.8 0.0 copy-done
  28.8 0.6 %copy.8 = f32[16,8,128]{2,1,0:T(8,128)} copy(f32[16,8,128]{2,1,0:T(8,128)S(1)} %copy-done) | data formatting | bytes 131072
Async XLA Ops:
  27.2 1.5 %copy-start = (f32[16,8,128]{2,1,0:T(8,128)S(1)}, f32[16,8,128]{2,1,0:T(8,128)}, u32[]{:S(2)}) copy-start(f32[16,8,128]{2,1,0:T(8,128)} %get-tuple-element.5) | copy-start | bytes 196612

commit v6 on v5

--- a/solution.py
+++ b/solution.py
@@ -191,7 +191,7 @@
 
 
 def kernel(wide, narrow, rhs, cond, guess, pressure, residual, *scratch):
-    (ins, corner_out, corner_in, side_in, p0, u0r, op0, a1, u1r, u1, op1, a2, own2, g2, u2, op2, a3, op3, down0, up0, down1, up1, down2, up2,
+    (ins, corner_out, corner_in, k_in, side_out, side_in, p0, u0r, op0, a1, u1r, u1, op1, a2, own2, g2, u2, op2, a3, op3, down0, up0, down1, up1, down2, up2,
      in_sem, send0, recv0, send1, recv1, send2, recv2) = scratch
     w = lax.axis_index("wide")
     n = lax.axis_index("narrow")
@@ -276,40 +276,92 @@
             good = zgood if good is None else good & zgood
         return good
 
-    sizes = [(0, dz, DEEP - dz) for dz in range(1, DEEP)]
-    sizes += [(2, dz, DEEP - dz) for dz in range(1, DEEP)]
-    sizes += [(1, dz, DEEP - 1 - dz) for dz in range(1, DEEP - 1)]
+    def mine_x(dw, dx):
+        return bx - dx if dw == 1 else dx - 1
+
+    def there_x(dw, dx):
+        return SIDE - dx if dw == -1 else SIDE + bx + dx - 1
+
+    def pairs(count):
+        return [tuple(range(dx, min(dx + 2, count + 1))) for dx in range(1, count + 1, 2)]
+
+    def run(dw, count, place):
+        return min(place(dw, 1), place(dw, count))
+
+    corners = [(-1, -1), (-1, 1), (1, -1), (1, 1)]
+    parts = [(0, dz, DEEP - dz) for dz in range(1, DEEP)] + [(1, dz, DEEP - 1 - dz) for dz in range(1, DEEP - 1)]
     slots = []
-    for which, dz, count in sizes:
-        slots.append((which, dz, count, sum(slot[2] for slot in slots)))
-    corners = [(-1, -1), (-1, 1), (1, -1), (1, 1)]
+    used = 0
+    for i, dz, count in parts:
+        slots.append((i, dz, count, used))
+        used += count
+    doubles = []
+    for dz in range(1, DEEP):
+        for pair in pairs(DEEP - dz):
+            doubles.append((dz, pair, used))
+            used += 1
 
     for c, (dw, dn) in enumerate(corners):
         for i, dz, count, at in slots:
             z = bz - dz if dn == 1 else dz - 1
-            x = bx - count if dw == 1 else 0
+            x = run(dw, count, mine_x)
             corner_out[c, at:at + count, :] = ins[i, x:x + count, z, :]
+        for dz, pair, at in doubles:
+            z = bz - dz if dn == 1 else dz - 1
+            x = mine_x(dw, pair[0])
+            row = ins[2, x, z:z + 1, :]
+            if len(pair) > 1:
+                odd = (iota((1, LANES), 1) + (x + z)) & 1
+                row = jnp.where(odd == 1, row, ins[2, mine_x(dw, pair[1]), z:z + 1, :])
+            corner_out[c, at:at + 1, :] = row
+
+    for d, dw in enumerate((-1, 1)):
+        x = run(dw, DEEP - 1, mine_x)
+        side_out[d, 0:DEEP - 1] = ins[1, x:x + DEEP - 1]
+        for at, pair in enumerate(pairs(DEEP)):
+            x = mine_x(dw, pair[0])
+            layer = ins[2, x]
+            if len(pair) > 1:
+                odd = (iota(layer.shape, 0) + iota(layer.shape, 1) + x) & 1
+                layer = jnp.where(odd == 1, layer, ins[2, mine_x(dw, pair[1])])
+            side_out[d, DEEP - 1 + at] = layer
 
     def corner_unpack(dw, dn):
         c = corners.index((-dw, -dn))
         for i, dz, count, at in slots:
             z = DEEP - dz if dn == -1 else DEEP + bz + dz - 1
-            x = SIDE - count if dw == -1 else SIDE + bx
+            x = run(dw, count, there_x)
             p0[i, z, x:x + count, :] = corner_in[c, at:at + count, :]
+        for dz, pair, at in doubles:
+            z = DEEP - dz if dn == -1 else DEEP + bz + dz - 1
+            for dx in pair:
+                x = there_x(dw, dx)
+                p0[2, z, x:x + 1, :] = corner_in[c, at:at + 1, :]
 
     def side_unpack(which, dw):
-        at = SIDE - DEEP if dw == -1 else SIDE + bx
-        for i in ((0,), (1, 2))[which]:
+        d = (dw + 1) // 2
+        if which == 0:
+            x = run(dw, DEEP, there_x)
             for z in range(bz):
-                p0[i, DEEP + z, at:at + DEEP, :] = side_in[(dw + 1) // 2, i, :, z, :]
+                p0[0, DEEP + z, x:x + DEEP, :] = k_in[d, :, z, :]
+            return
+        x = run(dw, DEEP - 1, there_x)
+        for z in range(bz):
+            p0[1, DEEP + z, x:x + DEEP - 1, :] = side_in[d, 0:DEEP - 1, z, :]
+        for at, pair in enumerate(pairs(DEEP)):
+            for dx in pair:
+                x = there_x(dw, dx)
+                p0[2, DEEP:DEEP + bz, x, :] = side_in[d, DEEP - 1 + at]
 
     def fine_refs(which, dw, dn):
         if which < 2 and dw and dn:
             c = corners.index((dw, dn))
             return corner_out.at[c], corner_in.at[c]
         arrays = (pl.ds(0, 1), pl.ds(1, 2), None)[which]
-        if which < 2 and dw:
-            return ins.at[arrays, pl.ds(bx - DEEP if dw == 1 else 0, DEEP)], side_in.at[(1 - dw) // 2, arrays]
+        if which == 0 and dw:
+            return ins.at[0, pl.ds(run(dw, DEEP, mine_x), DEEP)], k_in.at[(1 - dw) // 2]
+        if which == 1 and dw:
+            return side_out.at[(dw + 1) // 2], side_in.at[(1 - dw) // 2]
         src_z, dst_z, len_z = zs[dn]
         src_x, dst_x, len_x = xs[dw]
         ref = u0r if which == 2 else p0
@@ -546,15 +598,9 @@
         side = ((zi - DEEP) % 4) // 2
         p0[2, zi] = u0r[zi] + grown[span * t:span * (t + 1), LANES * side:LANES * (side + 1)]
     zero_level.smooth()
-    stores = [pltpu.make_async_copy(ins.at[i], ref, in_sem.at[i]) for i, ref in enumerate((pressure, residual))]
-    for z in range(bz):
-        ins[0, :, z, :] = p0[2, DEEP + z, SIDE:SIDE + bx, :]
-    stores[0].start()
     for z, left in enumerate(zero_level.defects(DEEP, DEEP + bz)):
-        ins[1, :, z, :] = left[SIDE:SIDE + bx]
-    stores[1].start()
-    for store in stores:
-        store.wait()
+        pressure[:, z, :] = p0[2, DEEP + z, SIDE:SIDE + bx, :]
+        residual[:, z, :] = left[SIDE:SIDE + bx]
 
 
 def local(wide, narrow, rhs, coefficient, guess):
@@ -568,6 +614,7 @@
     x2 = wide * bx // 4
     x3 = x2 // 2
     vmem = lambda *shape: pltpu.VMEM(shape, jnp.float32)
+    layers = DEEP - 1 + (DEEP + 1) // 2
     half = lambda *shape: pltpu.VMEM(shape, jnp.bfloat16)
     dma = lambda *shape: pltpu.SemaphoreType.DMA(shape)
     out = jax.ShapeDtypeStruct(rhs.shape, jnp.float32)
@@ -575,9 +622,10 @@
         functools.partial(kernel, wide, narrow),
         out_shape=(out, out),
         in_specs=[pl.BlockSpec(memory_space=pltpu.HBM)] * 3,
-        out_specs=[pl.BlockSpec(memory_space=pltpu.HBM)] * 2,
+        out_specs=[pl.BlockSpec(memory_space=pltpu.VMEM)] * 2,
         scratch_shapes=[
-            vmem(3, bx, bz, by), vmem(4, 32, LANES), vmem(4, 32, LANES), vmem(2, 3, DEEP, bz, by),
+            vmem(3, bx, bz, by), vmem(4, 24, LANES), vmem(4, 24, LANES),
+            vmem(2, DEEP, bz, by), vmem(2, layers, bz, by), vmem(2, layers, bz, by),
             vmem(3, z0, x0, by), vmem(z0, x0, by), vmem(6, z0, x0, by),
             vmem(2, t1, x1, LANES), vmem(t1, x1, LANES), vmem(t1 + 2 * PAD, x1, LANES), vmem(6, t1, x1, LANES),
             vmem(2, t2, x2, LANES), vmem(2, t2 * hx // 2, LANES), vmem(2, wide, t2 * hx // 2, LANES),
@@ -587,8 +635,8 @@
             half(t2 * LANES, LANES), half(LANES, t2 * LANES),
             dma(3), dma(3, 9), dma(3, 9), dma(3, 3), dma(3, 3), dma(2), dma(2),
         ],
-        compiler_params=pltpu.CompilerParams(collective_id=0, has_side_effects=True, vmem_limit_bytes=64 * 2**20 - 2**18),
-    )(rhs, coefficient, guess)
+        compiler_params=pltpu.CompilerParams(collective_id=0, has_side_effects=True, vmem_limit_bytes=48 * 2**20),
+    )(*[pltpu.with_memory_space_constraint(a, pltpu.HBM) for a in (rhs, coefficient, guess)])
 
 
 def solution(mesh):

time: 29.6 us -> 27.3 us (0.922)
  Pallas kernels: 26.6 us -> 25.2 us
  local copies, waits for them, and re-layouts: 2.14 us -> 1.26 us
    pallas_call x1, Pallas kernels: 26.6 us -> 25.2 us  [local(): pl.pallas_call(functools.partial(kernel, wide, narrow), out_shape=(out, o...]
    unnamed x4 -> x2, local copies, waits for them, and re-layouts: 2.14 us -> 1.26 us
where the time goes in v6:
time: 27.3 us; the launch traced here: 27.1 us
  Pallas kernels  25.2 us (92%)
  local copies, waits for them, and re-layouts  1.26 us (5%)
  between operations  0.64 us (2%)
    pallas_call x1, Pallas kernels, local(): pl.pallas_call(functools.partial(kernel, wide, narrow), out_shape=(out, o...  25.2 us
    unnamed x2, local copies, waits for them, and re-layouts  1.26 us

profile of v6, /device:TPU:0, one launch (start us, length us, event | category | flops | bytes accessed | tf_op | source)
XLA Modules:
  0.0 27.1 jit_solution(14518244497756187978)
XLA Ops:
  0.6 25.2 %shard_map.50 = (f32[16,8,128]{2,1,0:T(8,128)S(1)}, f32[16,8,128]{2,1,0:T(8,128)S(1)}) custom-call(f32[16,8,128]{2,1,0:T(8,128)} %rhs.1, f32[16,8,128]{2,1,0:T(8,128)} %cond.1, f32[16,8,128]{2,1,0:T(8,128)} %guess.1), custom_call_target="tpu_custom_call" | custom-call | tf_op jit(solution)/shard_map/pallas_call | solution.py:621
  25.8 0.6 %copy.7 = f32[16,8,128]{2,1,0:T(8,128)} copy(f32[16,8,128]{2,1,0:T(8,128)S(1)} %get-tuple-element.4) | data formatting | bytes 131072
  26.5 0.6 %copy.8 = f32[16,8,128]{2,1,0:T(8,128)} copy(f32[16,8,128]{2,1,0:T(8,128)S(1)} %get-tuple-element.5) | data formatting | bytes 131072
